TPU v7x, 128 devices: a whole 4x4x4 slice. The times are simulated.
128 devices in a mesh: dp: 32 (over x_hi, y, z), feat: 4 (over x_lo, core).
Axes of the slice: x: 4 (x_hi: 2, x_lo: 2; x = x_hi * 2 + x_lo), y: 4, z: 4, core: 2. Of those that a mesh axis runs over, the one named last changes fastest.
Arguments:
- view_a: bfloat16 [24576, 4096], P('dp', 'feat'), may hold values from -4000 to 4000, as said below
- view_b: bfloat16 [24576, 4096], P('dp', 'feat'), may hold values from -4000 to 4000, as said below
Outputs:
- loss: float32 [], replicated
- grad_a: bfloat16 [24576, 4096], P('dp', 'feat')
- grad_b: bfloat16 [24576, 4096], P('dp', 'feat')
Inputs may be any that keep to these rules, and one draw needn't show every extreme that they name: `view_a`: for every feature, the magnitude of its mean over all 24576 samples is at most 20 times its standard deviation over them, and that standard deviation is 0.5 or more. `view_b`: for every feature, the magnitude of its mean over all 24576 samples is at most 20 times its standard deviation over them, and that standard deviation is 0.5 or more.
All inputs are finite; a program needn't handle non-finite values.
Results may differ from a plain program's by a relative error of at most 0.0039.
Values may be sent and summed in bfloat16 or wider, within the bound.
No kernel may reach another device: no remote copies, remote signals or barrier semaphores. Data moves between devices by JAX's collectives and lax.ppermute only.
A program may use at most 128 MiB of HBM per device.

v0:
```python
import functools

import jax
import jax.numpy as jnp
from jax import lax
from jax.experimental import pallas as pl
from jax.experimental.pallas import tpu as pltpu
from jax.sharding import PartitionSpec as P

epsilon = 1e-05
off_weight = 0.0051
low = jnp.bfloat16
full = jnp.float32


def at_z(step):
    return "dp", lambda d: d // 4 * 4 + (d + step) % 4


def at_y(step):
    return "dp", lambda d: d // 16 * 16 + (d // 4 + step) % 4 * 4 + d % 4


def flip(bits):
    return "dp", lambda d: d ^ bits


def across_both(member):
    return member ^ (16 * 4 + 2)


core = ("feat", lambda f: f ^ 1)
chip = ("feat", lambda f: f ^ 2)


def stage(sends, after=()):
    held = lax.optimization_barrier(tuple(values for values, _ in sends) + tuple(after))
    received = []
    for values, (_, (axis, place)) in zip(held, sends):
        count = 128 if isinstance(axis, tuple) else lax.axis_size(axis)
        received.append(lax.ppermute(values, axis, [(d, place(d)) for d in range(count)]))
    return received


def together(sends):
    return list(lax.optimization_barrier(tuple(stage(sends))))


def share(values, groups=None):
    count = len(groups[0]) if groups else lax.axis_size("dp")
    pieces = jnp.broadcast_to(values[None], (count,) + values.shape)
    return lax.all_to_all(pieces, "dp", 0, 0, tiled=True, axis_index_groups=groups)


def combine(means, products, rows):
    mean = jnp.mean(means, axis=0)
    shift = means - mean
    shifts = jnp.stack((shift[:, 0] ** 2, shift[:, 1] ** 2, shift[:, 0] * shift[:, 1]), axis=1)
    return mean, jnp.sum(products + rows * shifts, axis=0)


def normalise_kernel(view_b, view_c, stats, out):
    width = view_b.shape[1]
    for index, view in enumerate((view_b, view_c)):
        mean = stats[2 * index : 2 * index + 1, :]
        inverse = stats[2 * index + 1 : 2 * index + 2, :]
        values = (view[...].astype(full) - mean) * inverse
        out[:, index * width : (index + 1) * width] = values.astype(low)


def normalise(view_b, view_c, stats):
    rows, width = view_b.shape
    return pl.pallas_call(
        normalise_kernel,
        grid=(rows // 256,),
        in_specs=[
            pl.BlockSpec((256, width), lambda i: (i, 0)),
            pl.BlockSpec((256, width), lambda i: (i, 0)),
            pl.BlockSpec((8, width), lambda i: (0, 0)),
        ],
        out_specs=pl.BlockSpec((256, 2 * width), lambda i: (i, 0)),
        out_shape=jax.ShapeDtypeStruct((rows, 2 * width), low),
        compiler_params=pltpu.CompilerParams(vmem_limit_bytes=32 * 2**20),
    )(view_b, view_c, stats)


def add_kernel(*refs):
    for index in range(4):
        refs[8 + index][...] = (
            refs[index][...].astype(full) + refs[4 + index][...].astype(full)
        ).astype(low)


def add_halves(blocks, received):
    rows, columns = received[0].shape
    halves = [pl.BlockSpec((rows, 512), lambda i, h=h: (h, i)) for h in (0, 1, 0, 1)]
    return pl.pallas_call(
        add_kernel,
        grid=(columns // 512,),
        in_specs=halves + [pl.BlockSpec((rows, 512), lambda i: (0, i))] * 4,
        out_specs=halves,
        out_shape=[jax.ShapeDtypeStruct(block.shape, low) for block in blocks],
        input_output_aliases={index: index for index in range(4)},
        compiler_params=pltpu.CompilerParams(vmem_limit_bytes=32 * 2**20),
    )(*blocks, *received)


small_cost = pl.CostEstimate(flops=1, bytes_accessed=1, transcendentals=0)
params = pltpu.CompilerParams(vmem_limit_bytes=48 * 2**20)
over_columns = (((1,), (1,)), ((), ()))


def whole(*shape):
    return pl.BlockSpec(shape, lambda *_: (0,) * len(shape))


def slope_kernel(place, total, received, diagonal, out, *, pairs):
    corr = add(total[...], received[...]) / pairs
    shape = corr.shape
    own = place[0]
    row = lax.broadcasted_iota(jnp.int32, shape, 1)
    on_diagonal = (lax.broadcasted_iota(jnp.int32, shape, 2) == own + row) & (
        lax.broadcasted_iota(jnp.int32, shape, 0) == 0
    )
    lane = lax.broadcasted_iota(jnp.int32, diagonal.shape, 1)
    rest = 1.0 - diagonal[...]
    rest = jnp.where((lane >= own) & (lane < own + shape[1]), rest * rest, 0.0)
    loss = jnp.sum(jnp.where(on_diagonal, 0.0, off_weight * corr * corr)) + jnp.sum(rest)
    loss = jnp.full((1, 1, 128), loss)
    high = loss.astype(low).astype(full)
    middle = (loss - high).astype(low).astype(full)
    slots = jnp.zeros(shape, full)
    for index, part in enumerate((high, middle, loss - high - middle)):
        slots = jnp.where(row == index, jnp.max(part), slots)
    out[...] = jnp.where(on_diagonal, slots, 2.0 * off_weight * corr).astype(low)


def slope_tiles(place, total, received, diagonal, pairs):
    shape = received.shape
    return pl.pallas_call(
        functools.partial(slope_kernel, pairs=pairs),
        grid_spec=pltpu.PrefetchScalarGridSpec(
            num_scalar_prefetch=1,
            grid=(1,),
            in_specs=[whole(*shape), whole(*shape), whole(1, diagonal.shape[1])],
            out_specs=whole(*shape),
        ),
        out_shape=jax.ShapeDtypeStruct(shape, low),
        compiler_params=params,
    )(place, total, received, diagonal)


def far_kernel(position, left, right, top, bottom):
    columns = left[:, pl.ds(pl.multiple_of(position[0] * 256, 256), 256)]
    part = lax.dot_general(
        columns, right[...], (((0,), (0,)), ((), ())), preferred_element_type=full
    ).astype(low)
    top[...] = part[:128]
    bottom[...] = part[128:]


def far_chunk(position, left, right):
    rows, width = left.shape
    columns = right.shape[1]
    return pl.pallas_call(
        far_kernel,
        grid_spec=pltpu.PrefetchScalarGridSpec(
            num_scalar_prefetch=1,
            grid=(columns // 512,),
            in_specs=[whole(rows, width), pl.BlockSpec((rows, 512), lambda i, p: (0, i))],
            out_specs=[pl.BlockSpec((128, 512), lambda i, p: (0, i))] * 2,
        ),
        out_shape=[jax.ShapeDtypeStruct((128, columns), low)] * 2,
        compiler_params=params,
    )(position.astype(jnp.int32).reshape(1), left, right)


def product_kernel(left, right, out):
    out[...] = jnp.dot(left[...], right[...], preferred_element_type=full).astype(out.dtype)


def times(left, right, kind):
    rows, depth = left.shape
    columns = right.shape[1]
    return pl.pallas_call(
        product_kernel,
        grid=(rows // 256,),
        in_specs=[pl.BlockSpec((256, depth), lambda i: (i, 0)), whole(depth, columns)],
        out_specs=pl.BlockSpec((256, columns), lambda i: (i, 0)),
        out_shape=jax.ShapeDtypeStruct((rows, columns), kind),
        compiler_params=params,
        cost_estimate=small_cost,
    )(left, right)


def upstream(even, odd, slope_even, slope_odd):
    up = lax.dot_general(even[...], slope_even[...], over_columns, preferred_element_type=full)
    return up + lax.dot_general(odd[...], slope_odd[...], over_columns, preferred_element_type=full)


def part_kernel(even, odd, slope_even, slope_odd, out):
    out[...] = upstream(even, odd, slope_even, slope_odd)


def grad_kernel(even, odd, slope_even, slope_odd, part, view, stats, out):
    up = part[...] + upstream(even, odd, slope_even, slope_odd)
    inverse = stats[1:2]
    norm = (view[...].astype(full) - stats[0:1]) * inverse
    out[...] = (inverse * (up - stats[3:4] - norm * stats[2:3])).astype(low)


def up_a_call(half, low_even, low_odd, slope_even, slope_odd, *more):
    rows = low_even.shape[0]
    width = slope_even.shape[0]
    left = pl.BlockSpec((256, width), lambda i: (i, half))
    tile = pl.BlockSpec((256, width), lambda i: (i, 0))
    square = whole(width, width)
    return pl.pallas_call(
        grad_kernel if more else part_kernel,
        grid=(rows // 256,),
        in_specs=[left, left, square, square] + ([tile, tile, whole(8, width)] if more else []),
        out_specs=tile,
        out_shape=jax.ShapeDtypeStruct((rows, width), low if more else full),
        compiler_params=params,
        cost_estimate=small_cost,
    )(low_even, low_odd, slope_even, slope_odd, *more)


def grad_b_kernel(left, slope, near, across, view, stats, out):
    up = jnp.dot(left[...], slope[...], preferred_element_type=full)
    up = up + near[...].astype(full) + across[...].astype(full)
    inverse = stats[1:2]
    norm = (view[...].astype(full) - stats[0:1]) * inverse
    out[...] = (inverse * (up - stats[3:4] - norm * stats[2:3])).astype(low)


def grad_b_call(left, slope, near, across, view, stats):
    rows, width = view.shape
    tile = pl.BlockSpec((256, width), lambda i: (i, 0))
    return pl.pallas_call(
        grad_b_kernel,
        grid=(rows // 256,),
        in_specs=[tile, whole(*slope.shape)] + [tile] * 3 + [whole(8, width)],
        out_specs=tile,
        out_shape=jax.ShapeDtypeStruct((rows, width), low),
        compiler_params=params,
        cost_estimate=small_cost,
    )(left, slope, near, across, view, stats)


def split_kernel(places, *refs):
    step = pl.program_id(0)
    for index in range(2):
        own, first, second = refs[3 * index : 3 * index + 3]
        total = own[...] + first[...].astype(full) + second[...].astype(full)
        for place in range(4):
            out = refs[6 + 4 * index + place]

            @pl.when(step == place)
            def _(out=out, total=total):
                out[...] = total.astype(out.dtype)


def split_sums(places, even, odd):
    rows, columns = even[0].shape
    size = rows // 4

    def block(index):
        return pl.BlockSpec((size, columns), lambda k, p: ((p[index] + k) & 3, 0))

    kinds = [full, low, low, low] * 2
    return pl.pallas_call(
        split_kernel,
        grid_spec=pltpu.PrefetchScalarGridSpec(
            num_scalar_prefetch=1,
            grid=(4,),
            in_specs=[block(0)] * 3 + [block(1)] * 3,
            out_specs=[whole(size, columns)] * 8,
        ),
        out_shape=[jax.ShapeDtypeStruct((size, columns), kind) for kind in kinds],
        compiler_params=params,
    )(places, *even, *odd)


def terms_kernel(slope, weights, means, diagonal_slope, columns, rows, *fixed):
    step = pl.program_id(0)

    @pl.when(step == 0)
    def _():
        columns[...] = jnp.zeros_like(columns)

    values = slope[...]
    if fixed:
        shape = values.shape
        on_diagonal = lax.broadcasted_iota(
            jnp.int32, shape, 1
        ) == step * 256 + lax.broadcasted_iota(jnp.int32, shape, 0)
        wide = values.astype(full)
        columns[2:3] += jnp.sum(jnp.where(on_diagonal, wide, 0.0), axis=0, keepdims=True)
        off = jnp.where(on_diagonal, 0.0, wide)
        values = jnp.where(on_diagonal, diagonal_slope[0:1], wide).astype(low)
        fixed[0][...] = values
    else:
        off = values.astype(full)
    squares = off * off * (0.5 / off_weight)
    columns[0:1] += jnp.sum(squares, axis=0, keepdims=True)
    columns[1:2] += jnp.dot(weights[...], values, preferred_element_type=full)[0:1]
    high = squares.astype(low)
    rest = (squares - high.astype(full)).astype(low)
    ones = jnp.ones((8, values.shape[1]), low)
    rows[0:1] = (
        lax.dot_general(ones, high, over_columns, preferred_element_type=full)
        + lax.dot_general(ones, rest, over_columns, preferred_element_type=full)
    )[0:1]
    rows[1:2] = lax.dot_general(means[...], values, over_columns, preferred_element_type=full)[0:1]
    rows[2:8] = jnp.zeros((6, 256), full)


def slope_terms(slope, weights, means, diagonal_slope=None):
    width = slope.shape[0]
    fix = diagonal_slope is not None
    tile = pl.BlockSpec((256, width), lambda i: (i, 0))
    outs = [jax.ShapeDtypeStruct((8, width), full)] * 2
    return pl.pallas_call(
        terms_kernel,
        grid=(4,),
        in_specs=[
            tile,
            pl.BlockSpec((16, 256), lambda i: (0, i)),
            whole(16, width),
            whole(8, width),
        ],
        out_specs=[whole(8, width), pl.BlockSpec((8, 256), lambda i: (0, i))] + [tile] * fix,
        out_shape=outs + [jax.ShapeDtypeStruct(slope.shape, low)] * fix,
        input_output_aliases={0: 2} if fix else {},
        compiler_params=params,
        cost_estimate=small_cost,
    )(slope, weights, means, diagonal_slope if fix else jnp.zeros((8, width), full))


def assemble_kernel(position, *refs):
    step = pl.program_id(0)
    out = refs[-1]
    halves = len(refs) == 6
    half = out.shape[0] // 2
    for index in range(4):

        @pl.when(step == index)
        def _(index=index):
            if halves and index == 1:
                out[:half] = refs[1][...]
                out[half:] = refs[2][...]
            else:
                out[...] = refs[index + halves * (index > 1)][...]


def add(one, other):
    return one.astype(full) + other.astype(full)


def pick(stack, index, axis):
    return lax.dynamic_index_in_dim(stack, index, axis, keepdims=False)


def put(stack, part, start):
    return lax.dynamic_update_slice_in_dim(stack, part, start, 0)


def around(block, place):
    return [(block, place(step)) for step in (2, 1, 3)]


def assemble(block, others, position):
    rows, columns = block.shape
    return pl.pallas_call(
        assemble_kernel,
        grid_spec=pltpu.PrefetchScalarGridSpec(
            num_scalar_prefetch=1,
            grid=(4,),
            in_specs=[whole(*part.shape) for part in (block, *others)],
            out_specs=pl.BlockSpec(
                (rows, columns),
                lambda k, p: ((p[0] - (k == 1) * 2 - (k == 2) * 1 - (k == 3) * 3) & 3, 0),
            ),
        ),
        out_shape=jax.ShapeDtypeStruct((4 * rows, columns), block.dtype),
        compiler_params=pltpu.CompilerParams(vmem_limit_bytes=32 * 2**20),
    )(position.astype(jnp.int32).reshape(1), block, *others)


def on_device(view_a, view_b):
    dp_count = lax.axis_size("dp")
    rows, width = view_a.shape
    pairs = rows * dp_count
    dp_index = lax.axis_index("dp")
    xi, yi, zi = dp_index >> 4, (dp_index >> 2) & 3, dp_index & 3
    view_c = stage([(view_b, chip)])[0]
    first = view_a.astype(full)
    second = view_b.astype(full)
    means = jnp.stack((jnp.mean(first, axis=0), jnp.mean(second, axis=0)))
    rest_a, rest_b = first - means[0], second - means[1]
    products = jnp.stack(
        (
            jnp.sum(rest_a * rest_a, axis=0),
            jnp.sum(rest_b * rest_b, axis=0),
            jnp.sum(rest_a * rest_b, axis=0),
        )
    )
    half_groups = [[16 * x + i for i in range(16)] for x in range(2)]
    shared = share(jnp.concatenate((means, products)).reshape(-1, 128), half_groups)
    shared = shared.reshape(16, 5, width)
    mean, products = combine(shared[:, :2], shared[:, 2:], rows)
    parts = jnp.concatenate((mean, products))
    part_b = jnp.stack((mean[1], products[1]))
    parts, part_b, view_c = lax.optimization_barrier((parts, part_b, view_c))
    other, part_c, part_d = stage(
        [(parts, flip(16)), (part_b, chip), (part_b, (("dp", "feat"), across_both))]
    )
    both = jnp.stack((parts, other))
    mean, products = combine(both[:, :2], both[:, 2:], pairs // 2)
    inverse = lax.rsqrt(products[:2] / pairs + epsilon)
    inv_a, inv_b = inverse
    diagonal = products[2] / pairs * inv_a * inv_b
    mean_c = 0.5 * (part_c[0] + part_d[0])
    products_c = part_c[1] + part_d[1] + (pairs // 4) * (part_c[0] - part_d[0]) ** 2
    inv_c = lax.rsqrt(products_c / pairs + epsilon)
    stats = jnp.concatenate(
        (jnp.stack((mean[1], inv_b, mean_c, inv_c)), jnp.zeros((4, width), full))
    )
    norm_a = (first - mean[0]) * inv_a
    low_a = norm_a.astype(low)

    low_even = normalise(view_b, view_c, stats)
    low_odd = stage([(low_even, core)])[0]
    ways = ((low_even, at_z, zi), (low_odd, at_y, yi))

    def product(right, start, size):
        columns = lax.dynamic_slice_in_dim(low_a, start, size, 1)
        return lax.dot_general(
            columns, right, (((0,), (0,)), ((), ())), preferred_element_type=full
        )

    sends = []
    for right, place, position in ways:
        top, bottom = far_chunk((position + 2) & 3, low_a, right)
        sends.extend(((top, place(1)), (bottom, place(3))))
    nears = [
        product(right, ((position + step) & 3) * 256, 256).astype(low)
        for right, _, position in ways
        for step in (1, 3)
    ]
    got = together(sends)
    nears = add_halves(nears, got)
    sends = [
        (near, place(step))
        for near, (place, step) in zip(nears, ((at_z, 1), (at_z, 3), (at_y, 1), (at_y, 3)))
    ]
    local = jnp.concatenate(
        (
            jnp.sum(low_a.astype(full), axis=0),
            jnp.sum(low_even.astype(full), axis=0),
            jnp.sum(low_odd.astype(full), axis=0),
        )
    )
    local = share(local.reshape(-1, 128))
    owns = [product(right, position * 256, 256) for right, _, position in ways]
    local, owns, got = lax.optimization_barrier((local, owns, tuple(stage(sends))))
    low_means = jnp.sum(local, axis=0).reshape(5, width) / pairs

    others = ((at_y, yi), (at_z, zi))
    blocks = split_sums(
        jnp.stack((yi, zi)).astype(jnp.int32), (owns[0], *got[:2]), (owns[1], *got[2:])
    )
    got = together(
        [
            (blocks[4 * index + step], place(step))
            for step in (2, 1, 3)
            for index, (place, _) in enumerate(others)
        ]
    )
    totals = jnp.stack(
        [
            sum((other.astype(full) for other in got[index::2]), blocks[4 * index]).astype(low)
            for index in range(2)
        ]
    )
    got = stage([(totals, flip(16))])[0]
    place = (zi * 256 + yi * 64).astype(jnp.int32).reshape(1)
    both = slope_tiles(place, totals, got, diagonal[None], pairs)
    got = together(
        [(both[index], place(step)) for step in (2, 1, 3) for index, (place, _) in enumerate(others)]
    )
    blocks = [
        assemble(both[index], got[index::2], position) for index, (_, position) in enumerate(others)
    ]

    diagonal_slope = (-2.0 * (1.0 - diagonal)).astype(low).astype(full)
    wide_slope = jnp.broadcast_to(diagonal_slope, (8, width))
    weights, *means = (jnp.broadcast_to(mean, (16, width)).astype(low) for mean in low_means)
    near_even, near_odd = blocks[0][:, width:], blocks[1][:, width:]
    got = together(around(near_even, at_z) + around(near_odd, at_y))
    slope_d = assemble(near_odd, got[3:], yi)
    slope_c = assemble(near_even, got[:3], zi)
    product_d = stage([(times(low_a, slope_d, low), core)])[0]
    across = add(times(low_a, slope_c, full), product_d).astype(low)
    near_even, near_odd = blocks[0][:, :width], blocks[1][:, :width]
    across, near_even, near_odd = lax.optimization_barrier((across, near_even, near_odd))
    across = stage([(across, chip)])[0]
    columns_c, rows_c = slope_terms(slope_c, weights, means[1])
    columns_d, rows_d = slope_terms(slope_d, weights, means[3])
    part_a = up_a_call(1, low_even, low_odd, slope_c, slope_d)
    got = stage(
        [(near_even, at_z(1)), (near_even, at_z(3)), (near_odd, at_y(1)), (near_odd, at_y(3))]
    )
    got, (columns_c, rows_c, columns_d, rows_d) = lax.optimization_barrier(
        (got, (columns_c, rows_c, columns_d, rows_d))
    )
    half = near_even.shape[0] // 2
    sends = [
        (got[0][:half], at_z(1)),
        (got[1][half:], at_z(3)),
        (got[2][:half], at_y(1)),
        (got[3][half:], at_y(3)),
    ]
    far, part_a = lax.optimization_barrier((tuple(stage(sends)), part_a))
    slope_e = assemble(near_odd, [*far[2:], *got[2:]], yi)
    slope_b = assemble(near_even, [*far[:2], *got[:2]], zi)
    near = times(low_a, slope_e, low)
    columns_b, rows_b, slope_b = slope_terms(slope_b, weights, means[0], wide_slope)
    columns_e, rows_e = slope_terms(slope_e, weights, means[2])
    loss = jnp.sum(columns_b[2].reshape(16, 64)[:, :3])
    loss_row = jnp.full((1, width), loss)
    small = jnp.concatenate((columns_e[:2], columns_d[:2], loss_row))
    across, near, small = lax.optimization_barrier((across, near, small))
    diagonal_term = diagonal_slope * diagonal
    near, small = stage([(near, core), (small, core)])
    distant = stage([(jnp.concatenate((columns_c[:2] + small[2:4], loss_row + small[4:5])), chip)])[0]
    rows_a = rows_b[:2] + rows_c[:2] + rows_d[:2] + rows_e[:2]
    rows_a = jnp.concatenate(((rows_a[0] + diagonal_term)[None], rows_a[1:2]))
    stats_a = jnp.concatenate((mean[0:1], inv_a[None], rows_a, jnp.zeros((4, width), full)))
    grad_a = up_a_call(0, low_even, low_odd, slope_b, slope_e, part_a, view_a, stats_a)
    grad_a, distant = lax.optimization_barrier((grad_a, distant))
    loss = loss + small[4, 0] + distant[2, 0]
    zeros = jnp.zeros((4, width), full)
    columns = columns_b[:2] + small[0:2] + distant[0:2]
    columns = jnp.concatenate(((columns[0] + diagonal_term)[None], columns[1:2]))
    stats_b = jnp.concatenate((mean[1:2], inv_b[None], columns, zeros))
    grad_b = grad_b_call(low_a, slope_b, near, across, view_b, stats_b)
    return (loss, grad_a, grad_b)


def solution(mesh):
    in_specs = (P("dp", "feat"), P("dp", "feat"))
    out_specs = (P(), P("dp", "feat"), P("dp", "feat"))
    return jax.shard_map(
        on_device, mesh=mesh, in_specs=in_specs, out_specs=out_specs, check_vma=False
    )
```

profile of v0, /device:TPU:0, one launch (start us, length us, event | category | flops | bytes accessed | tf_op | source)
XLA Modules:
  0.0 296.6 jit_solution(17759519622144273586)
XLA Ops:
  6.9 16.7 %all_to_all.10 = f32[16,40,128]{2,1,0:T(8,128)S(1)} all-to-all(f32[16,40,128]{2,1,0:T(8,128)S(1)} %broadcast_in_dim.41), channel_id=1, replica_groups={{0,4,8,12,16,20,24,28,32,36,40,44,48,52,56,60},{64,68,72,76,80,84,88,92..., dimensions={0} | all-to-all | bytes 655360 | tf_op jit(solution)/shard_map/all_to_all | solution.py:52
  24.2 12.7 %collective-permute-done.view_c = bf16[768,1024]{1,0:T(8,128)(2,1)S(1)} collective-permute-done((bf16[768,1024]{1,0:T(8,128)(2,1)}, bf16[768,1024]{1,0:T(8,128)(2,1)S(1)}, u32[]{:S(2)}, u32[]{:S(2)}) %collective-permute-start) | collective-permute-done | bytes 1572896 | tf_op jit(solution)/shard_map/ppermute | solution.py:41
  60.8 3.6 %shard_map.51 = (bf16[128,2048]{1,0:T(8,128)(2,1)S(1)}, bf16[128,2048]{1,0:T(8,128)(2,1)S(1)}) custom-call(s32[1]{0:T(128)} %bitcast.14.position, bf16[768,1024]{1,0:T(8,128)(2,1)S(1)} %get-tuple-element.233.left, bf16[768,2048]{1,0:T(8,128)(2,1)} %collective-permute-done.4.right.odd), custom_call_target="tpu_custom_call" | custom-call | tf_op jit(solution)/shard_map/pallas_call | solution.py:165
  71.8 3.9 %convolution_convert_fusion.refs_3_ = bf16[256,2048]{1,0:T(8,128)(2,1)} fusion(bf16[768,2048]{1,0:T(8,128)(2,1)} %collective-permute-done.4.right.odd, bf16[768,1024]{1,0:T(8,128)(2,1)S(1)} %get-tuple-element.233.left, s32[]{:T(128)S(6)} %select_n.23), kind=kOutput, calls=%fused_computation.17 | convolution fusion | flops 805830656 | bytes 4587524 | tf_op jit(solution)/shard_map/dot_general | solution.py:439
  75.8 3.9 %convolution_convert_fusion.1.refs_2_ = bf16[256,2048]{1,0:T(8,128)(2,1)} fusion(bf16[768,2048]{1,0:T(8,128)(2,1)} %collective-permute-done.4.right.odd, bf16[768,1024]{1,0:T(8,128)(2,1)S(1)} %get-tuple-element.233.left, s32[]{:T(128)S(6)} %select_n.22), kind=kOutput, calls=%fused_computation.18 | convolution fusion | flops 805830656 | bytes 4587524 | tf_op jit(solution)/shard_map/dot_general | solution.py:439
  83.1 3.9 %shard_map.52 = (bf16[256,2048]{1,0:T(8,128)(2,1)}, bf16[256,2048]{1,0:T(8,128)(2,1)}, bf16[256,2048]{1,0:T(8,128)(2,1)}, bf16[256,2048]{1,0:T(8,128)(2,1)}) custom-call(bf16[256,2048]{1,0:T(8,128)(2,1)} %convolution_convert_fusion.3.refs_0_, ...), custom_call_target="tpu_custom_call", output_to_operand_aliasing={{0}: (0, {}), {1}: (1, {}), {2}: (2, {}), {3}: (3, {})} | custom-call | tf_op jit(solution)/shard_map/pallas_call | solution.py:97
  95.8 5.9 %all-to-all-start.1 = ((f32[32,40,128]{2,1,0:T(8,128)}), f32[32,40,128]{2,1,0:T(8,128)}, u32[]{:S(2)}, u32[]{:S(2)}) async-start(f32[32,40,128]{2,1,0:T(8,128)} %broadcast_in_dim.43), calls=%async_computation.1 | async-start | bytes 1310720 | tf_op jit(solution)/shard_map/all_to_all | solution.py:52
  101.6 3.4 %fusion.14.refs_0_ = f32[256,2048]{1,0:T(8,128)} fusion(bf16[768,2048]{1,0:T(8,128)(2,1)S(1)} %shard_map.49.right.even, bf16[768,1024]{1,0:T(8,128)(2,1)} %copy-done.1, s32[]{:T(128)S(6)} %select_n.18), kind=kOutput, calls=%fused_computation.30 | convolution fusion | flops 805306368 | bytes 5636100 | tf_op jit(solution)/shard_map/dot_general | solution.py:439
  105.0 4.4 %fusion.12.refs_3_ = f32[256,2048]{1,0:T(8,128)} fusion(bf16[768,2048]{1,0:T(8,128)(2,1)} %collective-permute-done.4.right.odd, bf16[768,1024]{1,0:T(8,128)(2,1)} %copy-done.1, s32[]{:T(128)S(6)} %select_n.19), kind=kOutput, calls=%fused_computation.28 | convolution fusion | flops 805306368 | bytes 5636100 | tf_op jit(solution)/shard_map/dot_general | solution.py:439
  109.4 13.6 %all-to-all-done.1 = f32[32,40,128]{2,1,0:T(8,128)} async-done(((f32[32,40,128]{2,1,0:T(8,128)}), f32[32,40,128]{2,1,0:T(8,128)}, u32[]{:S(2)}, u32[]{:S(2)}) %all-to-all-start.1) | async-done | bytes 655392 | tf_op jit(solution)/shard_map/all_to_all | solution.py:52
  123.0 5.0 %shard_map.53 = (f32[64,2048]{1,0:T(8,128)S(1)}, bf16[64,2048]{1,0:T(8,128)(2,1)S(1)}, bf16[64,2048]{1,0:T(8,128)(2,1)S(1)}, bf16[64,2048]{1,0:T(8,128)(2,1)S(1)...) custom-call(s32[2]{0:T(128)S(1)} %pad_add_fusion.places, ...), custom_call_target="tpu_custom_call" | custom-call | tf_op jit(solution)/shard_map/pallas_call | solution.py:272
  140.1 3.1 %collective-permute-done.18 = bf16[64,2048]{1,0:T(8,128)(2,1)S(1)} collective-permute-done((bf16[64,2048]{1,0:T(8,128)(2,1)S(1)}, bf16[64,2048]{1,0:T(8,128)(2,1)S(1)}, u32[]{:S(2)}, u32[]{:S(2)}) %collective-permute-start.18) | collective-permute-done | bytes 262176 | tf_op jit(solution)/shard_map/ppermute | solution.py:41
  144.1 10.2 %collective-permute-done.19.received = bf16[2,64,2048]{2,1,0:T(8,128)(2,1)S(1)} collective-permute-done((bf16[2,64,2048]{2,1,0:T(8,128)(2,1)S(1)}, bf16[2,64,2048]{2,1,0:T(8,128)(2,1)S(1)}, u32[]{:S(2)}, u32[]{:S(2)}) %collective-permute-start.19) | collective-permute-done | bytes 524320 | tf_op jit(solution)/shard_map/ppermute | solution.py:41
  177.1 8.0 %collective-permute-start.30 = (bf16[256,1024]{1,0:T(8,128)(2,1)S(1)}, bf16[256,1024]{1,0:T(8,128)(2,1)S(1)}, u32[]{:S(2)}, u32[]{:S(2)}) collective-permute-start(bf16[256,1024]{1,0:T(8,128)(2,1)S(1)} %get-tuple-element.181.refs_0_), channel_id=1, source_target_pairs={{0,16},{4,20},{8,24},{12,28},{16,32},{20,36},{24,40},{28,44},{32,4... | collective-permute-start | bytes 1572872 | tf_op jit(solution)/shard_map/ppermute | solution.py:41
  187.0 12.5 %collective-permute-start.31 = (bf16[256,1024]{1,0:T(8,128)(2,1)S(1)}, bf16[256,1024]{1,0:T(8,128)(2,1)S(1)}, u32[]{:S(2)}, u32[]{:S(2)}) collective-permute-start(bf16[256,1024]{1,0:T(8,128)(2,1)S(1)} %get-tuple-element.181.refs_0_), channel_id=1, source_target_pairs={{0,48},{4,52},{8,56},{12,60},{16,0},{20,4},{24,8},{28,12},{32,16},... | collective-permute-start | bytes 1572872 | tf_op jit(solution)/shard_map/ppermute | solution.py:41
  199.5 8.1 %collective-permute-done.31.refs_3_ = bf16[256,1024]{1,0:T(8,128)(2,1)S(1)} collective-permute-done((bf16[256,1024]{1,0:T(8,128)(2,1)S(1)}, bf16[256,1024]{1,0:T(8,128)(2,1)S(1)}, u32[]{:S(2)}, u32[]{:S(2)}) %collective-permute-start.31) | collective-permute-done | bytes 524320 | tf_op jit(solution)/shard_map/ppermute | solution.py:41
  211.6 3.4 %shard_map.58 = f32[768,1024]{1,0:T(8,128)} custom-call(bf16[768,1024]{1,0:T(8,128)(2,1)S(1)} %copy-done.2, bf16[1024,1024]{1,0:T(8,128)(2,1)S(1)} %shard_map.57.right.slope.slope_even), custom_call_target="tpu_custom_call" | custom-call | flops 1 | bytes 1 | tf_op jit(solution)/shard_map/pallas_call | solution.py:185
  215.0 3.6 %add_convert_fusion = bf16[768,1024]{1,0:T(8,128)(2,1)} fusion(f32[768,1024]{1,0:T(8,128)} %shard_map.58, bf16[768,1024]{1,0:T(8,128)(2,1)S(1)} %collective-permute-done.32), kind=kLoop, calls=%fused_computation.15 | loop fusion | flops 2359296 | bytes 6291456 | tf_op jit(solution)/shard_map/convert_element_type | solution.py:505
  241.3 3.2 %collective-permute-start.38 = (bf16[128,1024]{1,0:T(8,128)(2,1)S(1)}, bf16[128,1024]{1,0:T(8,128)(2,1)S(1)}, u32[]{:S(2)}, u32[]{:S(2)}) collective-permute-start(bf16[128,1024]{1,0:T(8,128)(2,1)S(1)} %slice.193), channel_id=1, source_target_pairs={{0,12},{4,0},{8,4},{12,8},{16,28},{20,16},{24,20},{28,24},{32,44},... | collective-permute-start | bytes 786440 | tf_op jit(solution)/shard_map/ppermute | solution.py:41
  244.8 3.0 collective-permute-start.40
  247.8 6.3 %shard_map.63.part = f32[768,1024]{1,0:T(8,128)} custom-call(bf16[768,2048]{1,0:T(8,128)(2,1)} %copy-done, bf16[768,2048]{1,0:T(8,128)(2,1)} %collective-permute-done.4.right.odd, bf16[1024,1024]{1,0:T(8,128)(2,1)S(1)} %copy-done.7, bf16[1024,1024]{1,0:T(8,128)(2,1)S(1)} %copy-done.5), custom_call_target="tpu_custom_call" | custom-call | flops 1 | bytes 1 | tf_op jit(solution)/shard_map/pallas_call | solution.py:218
  263.2 4.0 %shard_map.65 = (f32[8,1024]{1,0:T(8,128)S(1)}, f32[8,1024]{1,0:T(8,128)S(1)}, bf16[1024,1024]{1,0:T(8,128)(2,1)S(1)}) custom-call(bf16[1024,1024]{1,0:T(8,128)(2,1)S(1)} %shard_map.64.slope, bf16[16,1024]{1,0:T(8,128)(2,1)S(1)} %broadcast_in_dim.44.weights, bf16[16,1024]{1,0:T(8,128)(2,1)S(1)} %broadcast_in_dim.47.means, ...), custom_call_target="tpu_custom_call", output_to_operand_aliasing={{2}: (0, {})} | custom-call | flops 1 | bytes 1 | tf_op jit(solution)/shard_map/pallas_call | solution.py:324
  278.8 6.8 %shard_map.69 = bf16[768,1024]{1,0:T(8,128)(2,1)} custom-call(bf16[768,2048]{1,0:T(8,128)(2,1)} %copy-done, bf16[768,2048]{1,0:T(8,128)(2,1)} %collective-permute-done.4.right.odd, bf16[1024,1024]{1,0:T(8,128)(2,1)S(1)} %copy-done.9, bf16[1024,1024]{1,0:T(8,128)(2,1)S(1)} %copy-done.11, f32[768,1024]{1,0:T(8,128)} %shard_map.63.part, ...), custom_call_target="tpu_custom_call" | custom-call | flops 1 | bytes 1 | tf_op jit(solution)/shard_map/pallas_call | solution.py:218
  288.7 6.6 %shard_map.70 = bf16[768,1024]{1,0:T(8,128)(2,1)} custom-call(bf16[768,1024]{1,0:T(8,128)(2,1)S(1)} %copy-done.2, bf16[1024,1024]{1,0:T(8,128)(2,1)} %copy-done.8, bf16[768,1024]{1,0:T(8,128)(2,1)} %collective-permute-done.44.near, bf16[768,1024]{1,0:T(8,128)(2,1)} %collective-permute-done.41.across, bf16[768,1024]{1,0:T(8,128)(2,1)} %view.3, ...), custom_call_target="tpu_custom_call" | custom-call | flops 1 | bytes 1 | tf_op jit(solution)/shard_map/pallas_call | solution.py:240
  (217 shorter events, 136.3 us)
Async XLA Ops:
  0.7 36.3 %collective-permute-start = (bf16[768,1024]{1,0:T(8,128)(2,1)}, bf16[768,1024]{1,0:T(8,128)(2,1)S(1)}, u32[]{:S(2)}, u32[]{:S(2)}) collective-permute-start(bf16[768,1024]{1,0:T(8,128)(2,1)} %view.3), channel_id=1, source_target_pairs={{0,2},{1,3},{2,0},{3,1},{4,6},{5,7},{6,4},{7,5},{8,10},{9,11},{10,... | collective-permute-start | bytes 4718600 | tf_op jit(solution)/shard_map/ppermute | solution.py:41
  64.4 15.8 %collective-permute-start.5 = (bf16[128,2048]{1,0:T(8,128)(2,1)S(1)}, bf16[128,2048]{1,0:T(8,128)(2,1)S(1)}, u32[]{:S(2)}, u32[]{:S(2)}) collective-permute-start(bf16[128,2048]{1,0:T(8,128)(2,1)S(1)} %get-tuple-element.126), channel_id=1, source_target_pairs={{0,4},{4,8},{8,12},{12,0},{16,20},{20,24},{24,28},{28,16},{32,36},... | collective-permute-start | bytes 1572872 | tf_op jit(solution)/shard_map/ppermute | solution.py:41
  66.4 13.8 %collective-permute-start.6 = (bf16[128,2048]{1,0:T(8,128)(2,1)S(1)}, bf16[128,2048]{1,0:T(8,128)(2,1)S(1)}, u32[]{:S(2)}, u32[]{:S(2)}) collective-permute-start(bf16[128,2048]{1,0:T(8,128)(2,1)S(1)} %get-tuple-element.127), channel_id=1, source_target_pairs={{0,12},{4,0},{8,4},{12,8},{16,28},{20,16},{24,20},{28,24},{32,44},... | collective-permute-start | bytes 1572872 | tf_op jit(solution)/shard_map/ppermute | solution.py:41
  68.6 14.4 %collective-permute-start.7 = (bf16[128,2048]{1,0:T(8,128)(2,1)S(1)}, bf16[128,2048]{1,0:T(8,128)(2,1)S(1)}, u32[]{:S(2)}, u32[]{:S(2)}) collective-permute-start(bf16[128,2048]{1,0:T(8,128)(2,1)S(1)} %get-tuple-element.128), channel_id=1, source_target_pairs={{0,16},{4,20},{8,24},{12,28},{16,32},{20,36},{24,40},{28,44},{32,4... | collective-permute-start | bytes 1572872 | tf_op jit(solution)/shard_map/ppermute | solution.py:41
  70.2 12.8 %collective-permute-start.8 = (bf16[128,2048]{1,0:T(8,128)(2,1)S(1)}, bf16[128,2048]{1,0:T(8,128)(2,1)S(1)}, u32[]{:S(2)}, u32[]{:S(2)}) collective-permute-start(bf16[128,2048]{1,0:T(8,128)(2,1)S(1)} %get-tuple-element.129), channel_id=1, source_target_pairs={{0,48},{4,52},{8,56},{12,60},{16,0},{20,4},{24,8},{28,12},{32,16},... | collective-permute-start | bytes 1572872 | tf_op jit(solution)/shard_map/ppermute | solution.py:41
  86.9 36.1 %collective-permute-start.10 = (bf16[256,2048]{1,0:T(8,128)(2,1)}, bf16[256,2048]{1,0:T(8,128)(2,1)}, u32[]{:S(2)}, u32[]{:S(2)}) collective-permute-start(bf16[256,2048]{1,0:T(8,128)(2,1)} %get-tuple-element.135), channel_id=1, source_target_pairs={{0,12},{4,0},{8,4},{12,8},{16,28},{20,16},{24,20},{28,24},{32,44},... | collective-permute-start | bytes 3145736 | tf_op jit(solution)/shard_map/ppermute | solution.py:41
  88.6 34.4 %collective-permute-start.11 = (bf16[256,2048]{1,0:T(8,128)(2,1)}, bf16[256,2048]{1,0:T(8,128)(2,1)}, u32[]{:S(2)}, u32[]{:S(2)}) collective-permute-start(bf16[256,2048]{1,0:T(8,128)(2,1)} %get-tuple-element.136), channel_id=1, source_target_pairs={{0,16},{4,20},{8,24},{12,28},{16,32},{20,36},{24,40},{28,44},{32,4... | collective-permute-start | bytes 3145736 | tf_op jit(solution)/shard_map/ppermute | solution.py:41
  90.1 32.9 %collective-permute-start.12 = (bf16[256,2048]{1,0:T(8,128)(2,1)}, bf16[256,2048]{1,0:T(8,128)(2,1)}, u32[]{:S(2)}, u32[]{:S(2)}) collective-permute-start(bf16[256,2048]{1,0:T(8,128)(2,1)} %get-tuple-element.137), channel_id=1, source_target_pairs={{0,48},{4,52},{8,56},{12,60},{16,0},{20,4},{24,8},{28,12},{32,16},... | collective-permute-start | bytes 3145736 | tf_op jit(solution)/shard_map/ppermute | solution.py:41
  92.1 30.9 %collective-permute-start.9 = (bf16[256,2048]{1,0:T(8,128)(2,1)}, bf16[256,2048]{1,0:T(8,128)(2,1)}, u32[]{:S(2)}, u32[]{:S(2)}) collective-permute-start(bf16[256,2048]{1,0:T(8,128)(2,1)} %get-tuple-element.134), channel_id=1, source_target_pairs={{0,4},{4,8},{8,12},{12,0},{16,20},{20,24},{24,28},{28,16},{32,36},... | collective-permute-start | bytes 3145736 | tf_op jit(solution)/shard_map/ppermute | solution.py:41
  95.8 27.3 %all-to-all-start.1 = ((f32[32,40,128]{2,1,0:T(8,128)}), f32[32,40,128]{2,1,0:T(8,128)}, u32[]{:S(2)}, u32[]{:S(2)}) async-start(f32[32,40,128]{2,1,0:T(8,128)} %broadcast_in_dim.43), calls=%async_computation.1 | async-start | bytes 1310720 | tf_op jit(solution)/shard_map/all_to_all | solution.py:52
  171.0 16.0 %collective-permute-start.26 = (bf16[256,1024]{1,0:T(8,128)(2,1)S(1)}, bf16[256,1024]{1,0:T(8,128)(2,1)S(1)}, u32[]{:S(2)}, u32[]{:S(2)}) collective-permute-start(bf16[256,1024]{1,0:T(8,128)(2,1)S(1)} %get-tuple-element.178.refs_0_), channel_id=1, source_target_pairs={{0,8},{4,12},{8,0},{12,4},{16,24},{20,28},{24,16},{28,20},{32,40},... | collective-permute-start | bytes 1572872 | tf_op jit(solution)/shard_map/ppermute | solution.py:41
  172.2 27.3 %collective-permute-start.27 = (bf16[256,1024]{1,0:T(8,128)(2,1)S(1)}, bf16[256,1024]{1,0:T(8,128)(2,1)S(1)}, u32[]{:S(2)}, u32[]{:S(2)}) collective-permute-start(bf16[256,1024]{1,0:T(8,128)(2,1)S(1)} %get-tuple-element.178.refs_0_), channel_id=1, source_target_pairs={{0,4},{4,8},{8,12},{12,0},{16,20},{20,24},{24,28},{28,16},{32,36},... | collective-permute-start | bytes 1572872 | tf_op jit(solution)/shard_map/ppermute | solution.py:41
  174.8 24.6 %collective-permute-start.28 = (bf16[256,1024]{1,0:T(8,128)(2,1)S(1)}, bf16[256,1024]{1,0:T(8,128)(2,1)S(1)}, u32[]{:S(2)}, u32[]{:S(2)}) collective-permute-start(bf16[256,1024]{1,0:T(8,128)(2,1)S(1)} %get-tuple-element.178.refs_0_), channel_id=1, source_target_pairs={{0,12},{4,0},{8,4},{12,8},{16,28},{20,16},{24,20},{28,24},{32,44},... | collective-permute-start | bytes 1572872 | tf_op jit(solution)/shard_map/ppermute | solution.py:41
  175.4 24.0 %collective-permute-start.29 = (bf16[256,1024]{1,0:T(8,128)(2,1)S(1)}, bf16[256,1024]{1,0:T(8,128)(2,1)S(1)}, u32[]{:S(2)}, u32[]{:S(2)}) collective-permute-start(bf16[256,1024]{1,0:T(8,128)(2,1)S(1)} %get-tuple-element.181.refs_0_), channel_id=1, source_target_pairs={{0,32},{4,36},{8,40},{12,44},{16,48},{20,52},{24,56},{28,60},{32,0... | collective-permute-start | bytes 1572872 | tf_op jit(solution)/shard_map/ppermute | solution.py:41
  177.1 22.4 %collective-permute-start.30 = (bf16[256,1024]{1,0:T(8,128)(2,1)S(1)}, bf16[256,1024]{1,0:T(8,128)(2,1)S(1)}, u32[]{:S(2)}, u32[]{:S(2)}) collective-permute-start(bf16[256,1024]{1,0:T(8,128)(2,1)S(1)} %get-tuple-element.181.refs_0_), channel_id=1, source_target_pairs={{0,16},{4,20},{8,24},{12,28},{16,32},{20,36},{24,40},{28,44},{32,4... | collective-permute-start | bytes 1572872 | tf_op jit(solution)/shard_map/ppermute | solution.py:41
  187.0 20.6 %collective-permute-start.31 = (bf16[256,1024]{1,0:T(8,128)(2,1)S(1)}, bf16[256,1024]{1,0:T(8,128)(2,1)S(1)}, u32[]{:S(2)}, u32[]{:S(2)}) collective-permute-start(bf16[256,1024]{1,0:T(8,128)(2,1)S(1)} %get-tuple-element.181.refs_0_), channel_id=1, source_target_pairs={{0,48},{4,52},{8,56},{12,60},{16,0},{20,4},{24,8},{28,12},{32,16},... | collective-permute-start | bytes 1572872 | tf_op jit(solution)/shard_map/ppermute | solution.py:41
  218.6 51.4 %collective-permute-start.41 = (bf16[768,1024]{1,0:T(8,128)(2,1)}, bf16[768,1024]{1,0:T(8,128)(2,1)}, u32[]{:S(2)}, u32[]{:S(2)}) collective-permute-start(bf16[768,1024]{1,0:T(8,128)(2,1)} %add_convert_fusion), channel_id=1, source_target_pairs={{0,2},{1,3},{2,0},{3,1},{4,6},{5,7},{6,4},{7,5},{8,10},{9,11},{10,... | collective-permute-start | bytes 4718600 | tf_op jit(solution)/shard_map/ppermute | solution.py:41
  218.9 16.8 %collective-permute-start.33 = (bf16[256,1024]{1,0:T(8,128)(2,1)S(1)}, bf16[256,1024]{1,0:T(8,128)(2,1)S(1)}, u32[]{:S(2)}, u32[]{:S(2)}) collective-permute-start(bf16[256,1024]{1,0:T(8,128)(2,1)S(1)} %get-tuple-element.191.refs_0_), channel_id=1, source_target_pairs={{0,4},{4,8},{8,12},{12,0},{16,20},{20,24},{24,28},{28,16},{32,36},... | collective-permute-start | bytes 1572872 | tf_op jit(solution)/shard_map/ppermute | solution.py:41
  220.0 15.8 %collective-permute-start.34 = (bf16[256,1024]{1,0:T(8,128)(2,1)S(1)}, bf16[256,1024]{1,0:T(8,128)(2,1)}, u32[]{:S(2)}, u32[]{:S(2)}) collective-permute-start(bf16[256,1024]{1,0:T(8,128)(2,1)S(1)} %get-tuple-element.191.refs_0_), channel_id=1, source_target_pairs={{0,12},{4,0},{8,4},{12,8},{16,28},{20,16},{24,20},{28,24},{32,44},... | collective-permute-start | bytes 1572872 | tf_op jit(solution)/shard_map/ppermute | solution.py:41
  222.6 15.1 %collective-permute-start.35 = (bf16[256,1024]{1,0:T(8,128)(2,1)S(1)}, bf16[256,1024]{1,0:T(8,128)(2,1)}, u32[]{:S(2)}, u32[]{:S(2)}) collective-permute-start(bf16[256,1024]{1,0:T(8,128)(2,1)S(1)} %get-tuple-element.193.refs_0_), channel_id=1, source_target_pairs={{0,16},{4,20},{8,24},{12,28},{16,32},{20,36},{24,40},{28,44},{32,4... | collective-permute-start | bytes 1572872 | tf_op jit(solution)/shard_map/ppermute | solution.py:41
  224.7 13.6 %collective-permute-start.36 = (bf16[256,1024]{1,0:T(8,128)(2,1)S(1)}, bf16[256,1024]{1,0:T(8,128)(2,1)}, u32[]{:S(2)}, u32[]{:S(2)}) collective-permute-start(bf16[256,1024]{1,0:T(8,128)(2,1)S(1)} %get-tuple-element.193.refs_0_), channel_id=1, source_target_pairs={{0,48},{4,52},{8,56},{12,60},{16,0},{20,4},{24,8},{28,12},{32,16},... | collective-permute-start | bytes 1572872 | tf_op jit(solution)/shard_map/ppermute | solution.py:41
  241.2 12.9 %collective-permute-start.37 = (bf16[128,1024]{1,0:T(8,128)(2,1)S(1)}, bf16[128,1024]{1,0:T(8,128)(2,1)S(1)}, u32[]{:S(2)}, u32[]{:S(2)}) collective-permute-start(bf16[128,1024]{1,0:T(8,128)(2,1)S(1)} %slice.192), channel_id=1, source_target_pairs={{0,4},{4,8},{8,12},{12,0},{16,20},{20,24},{24,28},{28,16},{32,36},... | collective-permute-start | bytes 786440 | tf_op jit(solution)/shard_map/ppermute | solution.py:41
  269.9 18.8 %collective-permute-start.44 = (bf16[768,1024]{1,0:T(8,128)(2,1)}, bf16[768,1024]{1,0:T(8,128)(2,1)}, u32[]{:S(2)}, u32[]{:S(2)}) collective-permute-start(bf16[768,1024]{1,0:T(8,128)(2,1)} %copy-done.18), channel_id=1, source_target_pairs={{0,1},{1,0},{2,3},{3,2},{4,5},{5,4},{6,7},{7,6},{8,9},{9,8},{10,11... | collective-permute-start | bytes 4718600 | tf_op jit(solution)/shard_map/ppermute | solution.py:41
  273.8 13.7 %collective-permute-start.43 = (f32[3,1024]{1,0:T(4,128)S(1)}, f32[3,1024]{1,0:T(4,128)S(1)}, u32[]{:S(2)}, u32[]{:S(2)}) collective-permute-start(f32[3,1024]{1,0:T(4,128)S(1)} %pad_maximum_fusion.5), channel_id=1, source_target_pairs={{0,2},{1,3},{2,0},{3,1},{4,6},{5,7},{6,4},{7,5},{8,10},{9,11},{10,... | collective-permute-start | bytes 36872 | tf_op jit(solution)/shard_map/ppermute | solution.py:41
  (45 other events, 424.3 us)
where the time goes:
time: 303 us; the launch traced here: 297 us
  starting transfers between devices  86.4 us (29%)
  waiting for transfers between devices  72.1 us (24%)
  Pallas kernels  59.5 us (20%)
  local copies, waits for them, and re-layouts  20.3 us (7%)
  matrix products  19.6 us (6%)
  other arithmetic  17.4 us (6%)
  blocking collectives  16.7 us (6%)
  between operations  4.68 us (2%)
    ppermute x45, starting transfers between devices, stage(): lax.ppermute(values, axis, [(d, place(d)) for d in range(count)])  80.5 us
    ppermute x45, waiting for transfers between devices, stage(): lax.ppermute(values, axis, [(d, place(d)) for d in range(count)])  58.5 us
    dot_general x6, matrix products, product(): lax.dot_general(columns, right, (((0,), (0,)), ((), ())), preferred_eleme...  19.6 us
    all_to_all x1, blocking collectives, share(): lax.all_to_all(pieces, 'dp', 0, 0, tiled=True, axis_index_groups=groups)  16.7 us
    unnamed x46, local copies, waits for them, and re-layouts  14.1 us
    all_to_all x1, waiting for transfers between devices, share(): lax.all_to_all(pieces, 'dp', 0, 0, tiled=True, axis_index_groups=groups)  13.6 us
    pallas_call x2, Pallas kernels, up_a_call(): pl.pallas_call(grad_kernel if more else part_kernel, grid=(rows // 256,),...  13.1 us
    pallas_call x4, Pallas kernels, slope_terms(): pl.pallas_call(terms_kernel, grid=(4,), in_specs=[tile, pl.BlockSpec((16,...  12.2 us
  transfers between devices with their start and end apart: 46, of which 20 were waited for; matrix products, arithmetic and copies ran while one was open for 13% of the time, Pallas kernels for 12%

commit v1 on v0

--- a/solution.py
+++ b/solution.py
@@ -159,6 +159,33 @@
     bottom[...] = part[128:]
 
 
+def near_kernel(position, left, right, above, below):
+    for step, out in ((1, above), (3, below)):
+        start = pl.multiple_of(((position[0] + step) & 3) * 256, 256)
+        out[...] = lax.dot_general(
+            left[:, pl.ds(start, 256)],
+            right[...],
+            (((0,), (0,)), ((), ())),
+            preferred_element_type=full,
+        ).astype(low)
+
+
+def near_chunks(position, left, right):
+    rows, width = left.shape
+    columns = right.shape[1]
+    return pl.pallas_call(
+        near_kernel,
+        grid_spec=pltpu.PrefetchScalarGridSpec(
+            num_scalar_prefetch=1,
+            grid=(columns // 512,),
+            in_specs=[whole(rows, width), pl.BlockSpec((rows, 512), lambda i, p: (0, i))],
+            out_specs=[pl.BlockSpec((256, 512), lambda i, p: (0, i))] * 2,
+        ),
+        out_shape=[jax.ShapeDtypeStruct((256, columns), low)] * 2,
+        compiler_params=params,
+    )(position.astype(jnp.int32).reshape(1), left, right)
+
+
 def far_chunk(position, left, right):
     rows, width = left.shape
     columns = right.shape[1]
@@ -212,18 +239,38 @@
 def up_a_call(half, low_even, low_odd, slope_even, slope_odd, *more):
     rows = low_even.shape[0]
     width = slope_even.shape[0]
-    left = pl.BlockSpec((256, width), lambda i: (i, half))
-    tile = pl.BlockSpec((256, width), lambda i: (i, 0))
-    square = whole(width, width)
+    left = pl.BlockSpec((rows, width), lambda i: (0, half))
+    right = pl.BlockSpec((256, width), lambda i: (i, 0))
+    tile = pl.BlockSpec((rows, 256), lambda i: (0, i))
+    line = pl.BlockSpec((8, 256), lambda i: (0, i))
     return pl.pallas_call(
         grad_kernel if more else part_kernel,
-        grid=(rows // 256,),
-        in_specs=[left, left, square, square] + ([tile, tile, whole(8, width)] if more else []),
+        grid=(width // 256,),
+        in_specs=[left, left, right, right] + ([tile, tile, line] if more else []),
         out_specs=tile,
         out_shape=jax.ShapeDtypeStruct((rows, width), low if more else full),
         compiler_params=params,
         cost_estimate=small_cost,
     )(low_even, low_odd, slope_even, slope_odd, *more)
+
+
+def halves_kernel(*refs):
+    for index in range(4):
+        refs[4 + index][...] = refs[index][...]
+
+
+def halves(blocks):
+    rows, columns = blocks[0].shape
+    return pl.pallas_call(
+        halves_kernel,
+        grid=(2,),
+        in_specs=[
+            pl.BlockSpec((rows // 2, columns // 2), lambda i, h=h: (h, i)) for h in (0, 1, 0, 1)
+        ],
+        out_specs=[pl.BlockSpec((rows // 2, columns // 2), lambda i: (0, i))] * 4,
+        out_shape=[jax.ShapeDtypeStruct((rows // 2, columns), low)] * 4,
+        compiler_params=params,
+    )(*blocks)
 
 
 def grad_b_kernel(left, slope, near, across, view, stats, out):
@@ -412,9 +459,15 @@
     mean, products = combine(shared[:, :2], shared[:, 2:], rows)
     parts = jnp.concatenate((mean, products))
     part_b = jnp.stack((mean[1], products[1]))
-    parts, part_b, view_c = lax.optimization_barrier((parts, part_b, view_c))
-    other, part_c, part_d = stage(
-        [(parts, flip(16)), (part_b, chip), (part_b, (("dp", "feat"), across_both))]
+    view_d = stage([(view_b, core)])[0]
+    parts, part_b, view_c, view_d = lax.optimization_barrier((parts, part_b, view_c, view_d))
+    other, part_c, part_d, view_e = together(
+        [
+            (parts, flip(16)),
+            (part_b, chip),
+            (part_b, (("dp", "feat"), across_both)),
+            (view_c, core),
+        ]
     )
     both = jnp.stack((parts, other))
     mean, products = combine(both[:, :2], both[:, 2:], pairs // 2)
@@ -431,7 +484,7 @@
     low_a = norm_a.astype(low)
 
     low_even = normalise(view_b, view_c, stats)
-    low_odd = stage([(low_even, core)])[0]
+    low_odd = normalise(view_d, view_e, stage([(stats, core)])[0])
     ways = ((low_even, at_z, zi), (low_odd, at_y, yi))
 
     def product(right, start, size):
@@ -445,9 +498,7 @@
         top, bottom = far_chunk((position + 2) & 3, low_a, right)
         sends.extend(((top, place(1)), (bottom, place(3))))
     nears = [
-        product(right, ((position + step) & 3) * 256, 256).astype(low)
-        for right, _, position in ways
-        for step in (1, 3)
+        near for right, _, position in ways for near in near_chunks(position, low_a, right)
     ]
     got = together(sends)
     nears = add_halves(nears, got)
@@ -462,10 +513,10 @@
             jnp.sum(low_odd.astype(full), axis=0),
         )
     )
-    local = share(local.reshape(-1, 128))
+    local = share(local.reshape(-1, 128), half_groups)
     owns = [product(right, position * 256, 256) for right, _, position in ways]
     local, owns, got = lax.optimization_barrier((local, owns, tuple(stage(sends))))
-    low_means = jnp.sum(local, axis=0).reshape(5, width) / pairs
+    local = jnp.sum(local, axis=0)
 
     others = ((at_y, yi), (at_z, zi))
     blocks = split_sums(
@@ -484,7 +535,8 @@
             for index in range(2)
         ]
     )
-    got = stage([(totals, flip(16))])[0]
+    got, other_local = together([(totals, flip(16)), (local, flip(16))])
+    low_means = (local + other_local).reshape(5, width) / pairs
     place = (zi * 256 + yi * 64).astype(jnp.int32).reshape(1)
     both = slope_tiles(place, totals, got, diagonal[None], pairs)
     got = together(
@@ -515,13 +567,7 @@
     got, (columns_c, rows_c, columns_d, rows_d) = lax.optimization_barrier(
         (got, (columns_c, rows_c, columns_d, rows_d))
     )
-    half = near_even.shape[0] // 2
-    sends = [
-        (got[0][:half], at_z(1)),
-        (got[1][half:], at_z(3)),
-        (got[2][:half], at_y(1)),
-        (got[3][half:], at_y(3)),
-    ]
+    sends = list(zip(halves(got), (at_z(1), at_z(3), at_y(1), at_y(3))))
     far, part_a = lax.optimization_barrier((tuple(stage(sends)), part_a))
     slope_e = assemble(near_odd, [*far[2:], *got[2:]], yi)
     slope_b = assemble(near_even, [*far[:2], *got[:2]], zi)

time: 303 us -> 284 us (0.937); the launches traced: 297 us -> 282 us
  Pallas kernels: 59.5 us -> 74.5 us
  matrix products: 19.6 us -> 5.73 us
  local copies, waits for them, and re-layouts: 20.3 us -> 12.7 us
  other arithmetic: 17.4 us -> 12.6 us
    dot_general x6 -> x2, matrix products: 19.6 us -> 5.73 us  [product(): lax.dot_general(columns, right, (((0,), (0,)), ((), ())), preferred_eleme...]
    pallas_call x2 -> x5, Pallas kernels: 13.1 us -> 24.8 us  [the longest x2 14.3 us: up_a_call(): pl.pallas_call(grad_kernel if more else part_kernel, grid=(width // 256,)...]
    pallas_call x1 -> x2, Pallas kernels: 0.77 us -> 5.59 us  [normalise(): pl.pallas_call(normalise_kernel, grid=(rows // 256,), in_specs=[pl.BlockS...]
    unnamed x46 -> x36, local copies, waits for them, and re-layouts: 14.1 us -> 9.63 us
    ppermute x45 -> x48, starting transfers between devices: 80.5 us -> 80 us  [stage(): lax.ppermute(values, axis, [(d, place(d)) for d in range(count)])]
    ppermute x45 -> x48, waiting for transfers between devices: 58.5 us -> 58.4 us  [stage(): lax.ppermute(values, axis, [(d, place(d)) for d in range(count)])]
  transfers between devices with their start and end apart: 46 -> 49, of which waited for: 20 -> 23; matrix products, arithmetic and copies ran while one was open for 13% -> 5% of each run, Pallas kernels for 12% -> 17%
where the time goes in v1:
time: 284 us; the launch traced here: 282 us
  starting transfers between devices  83.6 us (29%)
  Pallas kernels  74.5 us (26%)
  waiting for transfers between devices  70.7 us (25%)
  blocking collectives  17.7 us (6%)
  local copies, waits for them, and re-layouts  12.7 us (4%)
  other arithmetic  12.6 us (4%)
  matrix products  5.73 us (2%)
  between operations  4.38 us (2%)
    ppermute x48, starting transfers between devices, stage(): lax.ppermute(values, axis, [(d, place(d)) for d in range(count)])  80 us
    ppermute x48, waiting for transfers between devices, stage(): lax.ppermute(values, axis, [(d, place(d)) for d in range(count)])  58.4 us
    all_to_all x1, blocking collectives, share(): lax.all_to_all(pieces, 'dp', 0, 0, tiled=True, axis_index_groups=groups)  17.7 us
    pallas_call x2, Pallas kernels, up_a_call(): pl.pallas_call(grad_kernel if more else part_kernel, grid=(width // 256,)...  14.3 us
    pallas_call x4, Pallas kernels, slope_terms(): pl.pallas_call(terms_kernel, grid=(4,), in_specs=[tile, pl.BlockSpec((16,...  12.3 us
    all_to_all x1, waiting for transfers between devices, share(): lax.all_to_all(pieces, 'dp', 0, 0, tiled=True, axis_index_groups=groups)  12.3 us
    pallas_call x2, Pallas kernels, near_chunks(): pl.pallas_call(near_kernel, grid_spec=pltpu.PrefetchScalarGridSpec(num_sc...  10.1 us
    unnamed x36, local copies, waits for them, and re-layouts  9.63 us
  transfers between devices with their start and end apart: 49, of which 23 were waited for; matrix products, arithmetic and copies ran while one was open for 5% of the time, Pallas kernels for 17%

profile of v1, /device:TPU:0, one launch (start us, length us, event | category | flops | bytes accessed | tf_op | source)
XLA Modules:
  0.0 281.8 jit_solution(14384917860090126140)
XLA Ops:
  5.5 17.7 %all_to_all.10 = f32[16,40,128]{2,1,0:T(8,128)S(1)} all-to-all(f32[16,40,128]{2,1,0:T(8,128)S(1)} %broadcast_in_dim.41), channel_id=1, replica_groups={{0,4,8,12,16,20,24,28,32,36,40,44,48,52,56,60},{64,68,72,76,80,84,88,92..., dimensions={0} | all-to-all | bytes 655360 | tf_op jit(solution)/shard_map/all_to_all | solution.py:52
  23.7 13.3 %collective-permute-done.view_c = bf16[768,1024]{1,0:T(8,128)(2,1)} collective-permute-done((bf16[768,1024]{1,0:T(8,128)(2,1)}, bf16[768,1024]{1,0:T(8,128)(2,1)}, u32[]{:S(2)}, u32[]{:S(2)}) %collective-permute-start) | collective-permute-done | bytes 1572896 | tf_op jit(solution)/shard_map/ppermute | solution.py:41
  37.0 3.3 %collective-permute-start.2 = (f32[5,1024]{1,0:T(8,128)S(1)}, f32[5,1024]{1,0:T(8,128)S(1)}, u32[]{:S(2)}, u32[]{:S(2)}) collective-permute-start(f32[5,1024]{1,0:T(8,128)S(1)} %pad_maximum_fusion.2), channel_id=1, source_target_pairs={{0,64},{4,68},{8,72},{12,76},{16,80},{20,84},{24,88},{28,92},{32,9... | collective-permute-start | bytes 61448 | tf_op jit(solution)/shard_map/ppermute | solution.py:41
  57.7 3.3 %shard_map.54 = (bf16[128,2048]{1,0:T(8,128)(2,1)}, bf16[128,2048]{1,0:T(8,128)(2,1)}) custom-call(s32[1]{0:T(128)} %bitcast.14.position, bf16[768,1024]{1,0:T(8,128)(2,1)S(1)} %get-tuple-element.261.left, bf16[768,2048]{1,0:T(8,128)(2,1)S(1)} %shard_map.50.right.odd), custom_call_target="tpu_custom_call" | custom-call | tf_op jit(solution)/shard_map/pallas_call | solution.py:192
  68.2 5.1 %shard_map.51 = (bf16[256,2048]{1,0:T(8,128)(2,1)}, bf16[256,2048]{1,0:T(8,128)(2,1)}) custom-call(s32[1]{0:T(128)} %bitcast.position, bf16[768,1024]{1,0:T(8,128)(2,1)S(1)} %get-tuple-element.261.left, bf16[768,2048]{1,0:T(8,128)(2,1)} %copy-done), custom_call_target="tpu_custom_call" | custom-call | tf_op jit(solution)/shard_map/pallas_call | solution.py:176
  73.3 5.1 %shard_map.52 = (bf16[256,2048]{1,0:T(8,128)(2,1)}, bf16[256,2048]{1,0:T(8,128)(2,1)}) custom-call(s32[1]{0:T(128)} %bitcast.10.position, bf16[768,1024]{1,0:T(8,128)(2,1)S(1)} %get-tuple-element.261.left, bf16[768,2048]{1,0:T(8,128)(2,1)} %copy-done.2), custom_call_target="tpu_custom_call" | custom-call | tf_op jit(solution)/shard_map/pallas_call | solution.py:176
  83.4 4.1 %shard_map.55 = (bf16[256,2048]{1,0:T(8,128)(2,1)}, bf16[256,2048]{1,0:T(8,128)(2,1)}, bf16[256,2048]{1,0:T(8,128)(2,1)}, bf16[256,2048]{1,0:T(8,128)(2,1)}) custom-call(bf16[256,2048]{1,0:T(8,128)(2,1)} %get-tuple-element.142.refs_0_, ...), custom_call_target="tpu_custom_call", output_to_operand_aliasing={{0}: (0, {}), {1}: (1, {}), {2}: (2, {}), {3}: (3, {})} | custom-call | tf_op jit(solution)/shard_map/pallas_call | solution.py:97
  87.6 3.2 %collective-permute-start.12 = (bf16[256,2048]{1,0:T(8,128)(2,1)}, bf16[256,2048]{1,0:T(8,128)(2,1)}, u32[]{:S(2)}, u32[]{:S(2)}) collective-permute-start(bf16[256,2048]{1,0:T(8,128)(2,1)} %get-tuple-element.159), channel_id=1, source_target_pairs={{0,12},{4,0},{8,4},{12,8},{16,28},{20,16},{24,20},{28,24},{32,44},... | collective-permute-start | bytes 3145736 | tf_op jit(solution)/shard_map/ppermute | solution.py:41
  90.8 3.2 %collective-permute-start.14 = (bf16[256,2048]{1,0:T(8,128)(2,1)}, bf16[256,2048]{1,0:T(8,128)(2,1)}, u32[]{:S(2)}, u32[]{:S(2)}) collective-permute-start(bf16[256,2048]{1,0:T(8,128)(2,1)} %get-tuple-element.161), channel_id=1, source_target_pairs={{0,48},{4,52},{8,56},{12,60},{16,0},{20,4},{24,8},{28,12},{32,16},... | collective-permute-start | bytes 3145736 | tf_op jit(solution)/shard_map/ppermute | solution.py:41
  99.6 3.5 %all-to-all-start.1 = ((f32[16,40,128]{2,1,0:T(8,128)}), f32[16,40,128]{2,1,0:T(8,128)S(1)}, u32[]{:S(2)}, u32[]{:S(2)}) async-start(f32[16,40,128]{2,1,0:T(8,128)} %broadcast_in_dim.43), calls=%async_computation.1 | async-start | bytes 655360 | tf_op jit(solution)/shard_map/all_to_all | solution.py:52
  103.2 3.3 %fusion.8.refs_3_ = f32[256,2048]{1,0:T(8,128)} fusion(bf16[768,2048]{1,0:T(8,128)(2,1)S(1)} %copy-done.4, bf16[768,1024]{1,0:T(8,128)(2,1)} %copy-done.5, s32[]{:T(128)S(6)} %select_n.7), kind=kOutput, calls=%fused_computation.20 | convolution fusion | flops 805306368 | bytes 5636100 | tf_op jit(solution)/shard_map/dot_general | solution.py:492
  106.5 12.3 %all-to-all-done.1 = f32[16,40,128]{2,1,0:T(8,128)S(1)} async-done(((f32[16,40,128]{2,1,0:T(8,128)}), f32[16,40,128]{2,1,0:T(8,128)S(1)}, u32[]{:S(2)}, u32[]{:S(2)}) %all-to-all-start.1) | async-done | bytes 327712 | tf_op jit(solution)/shard_map/all_to_all | solution.py:52
  118.8 5.0 %shard_map.56 = (f32[64,2048]{1,0:T(8,128)S(1)}, bf16[64,2048]{1,0:T(8,128)(2,1)S(1)}, bf16[64,2048]{1,0:T(8,128)(2,1)S(1)}, bf16[64,2048]{1,0:T(8,128)(2,1)S(1)...) custom-call(s32[2]{0:T(128)S(1)} %pad_add_fusion.places, ...), custom_call_target="tpu_custom_call" | custom-call | tf_op jit(solution)/shard_map/pallas_call | solution.py:319
  133.2 3.4 %collective-permute-start.20 = (bf16[64,2048]{1,0:T(8,128)(2,1)S(1)}, bf16[64,2048]{1,0:T(8,128)(2,1)S(1)}, u32[]{:S(2)}, u32[]{:S(2)}) collective-permute-start(bf16[64,2048]{1,0:T(8,128)(2,1)S(1)} %get-tuple-element.180), channel_id=1, source_target_pairs={{0,12},{4,0},{8,4},{12,8},{16,28},{20,16},{24,20},{28,24},{32,44},... | collective-permute-start | bytes 786440 | tf_op jit(solution)/shard_map/ppermute | solution.py:41
  146.4 8.6 %collective-permute-done.22 = f32[40,128]{1,0:T(8,128)S(1)} collective-permute-done((f32[40,128]{1,0:T(8,128)S(1)}, f32[40,128]{1,0:T(8,128)S(1)}, u32[]{:S(2)}, u32[]{:S(2)}) %collective-permute-start.22) | collective-permute-done | bytes 20512 | tf_op jit(solution)/shard_map/ppermute | solution.py:41
  176.2 7.5 %collective-permute-start.32 = (bf16[256,1024]{1,0:T(8,128)(2,1)S(1)}, bf16[256,1024]{1,0:T(8,128)(2,1)S(1)}, u32[]{:S(2)}, u32[]{:S(2)}) collective-permute-start(bf16[256,1024]{1,0:T(8,128)(2,1)S(1)} %get-tuple-element.209.refs_0_), channel_id=1, source_target_pairs={{0,32},{4,36},{8,40},{12,44},{16,48},{20,52},{24,56},{28,60},{32,0... | collective-permute-start | bytes 1572872 | tf_op jit(solution)/shard_map/ppermute | solution.py:41
  187.5 3.7 %collective-permute-start.34 = (bf16[256,1024]{1,0:T(8,128)(2,1)S(1)}, bf16[256,1024]{1,0:T(8,128)(2,1)S(1)}, u32[]{:S(2)}, u32[]{:S(2)}) collective-permute-start(bf16[256,1024]{1,0:T(8,128)(2,1)S(1)} %get-tuple-element.209.refs_0_), channel_id=1, source_target_pairs={{0,48},{4,52},{8,56},{12,60},{16,0},{20,4},{24,8},{28,12},{32,16},... | collective-permute-start | bytes 1572872 | tf_op jit(solution)/shard_map/ppermute | solution.py:41
  201.4 3.4 %shard_map.61 = f32[768,1024]{1,0:T(8,128)} custom-call(bf16[768,1024]{1,0:T(8,128)(2,1)S(1)} %copy-done.6, bf16[1024,1024]{1,0:T(8,128)(2,1)S(1)} %shard_map.60.right.slope.slope_even), custom_call_target="tpu_custom_call" | custom-call | flops 1 | bytes 1 | tf_op jit(solution)/shard_map/pallas_call | solution.py:212
  204.8 3.6 %add_convert_fusion = bf16[768,1024]{1,0:T(8,128)(2,1)} fusion(f32[768,1024]{1,0:T(8,128)} %shard_map.61, bf16[768,1024]{1,0:T(8,128)(2,1)S(1)} %collective-permute-done.35), kind=kLoop, calls=%fused_computation.15 | loop fusion | flops 2359296 | bytes 6291456 | tf_op jit(solution)/shard_map/convert_element_type | solution.py:557
  212.0 3.4 %collective-permute-start.39 = (bf16[256,1024]{1,0:T(8,128)(2,1)S(1)}, bf16[256,1024]{1,0:T(8,128)(2,1)S(1)}, u32[]{:S(2)}, u32[]{:S(2)}) collective-permute-start(bf16[256,1024]{1,0:T(8,128)(2,1)S(1)} %get-tuple-element.221.refs_0_), channel_id=1, source_target_pairs={{0,48},{4,52},{8,56},{12,60},{16,0},{20,4},{24,8},{28,12},{32,16},... | collective-permute-start | bytes 1572872 | tf_op jit(solution)/shard_map/ppermute | solution.py:41
  234.2 6.9 %shard_map.67.part = f32[768,1024]{1,0:T(8,128)} custom-call(bf16[768,2048]{1,0:T(8,128)(2,1)} %copy-done, bf16[768,2048]{1,0:T(8,128)(2,1)} %copy-done.2, bf16[1024,1024]{1,0:T(8,128)(2,1)S(1)} %shard_map.60.right.slope.slope_even, bf16[1024,1024]{1,0:T(8,128)(2,1)S(1)} %shard_map.62.right.slope.slope_odd), custom_call_target="tpu_custom_call" | custom-call | flops 1 | bytes 1 | tf_op jit(solution)/shard_map/pallas_call | solution.py:246
  247.9 4.0 %shard_map.69 = (f32[8,1024]{1,0:T(8,128)S(1)}, f32[8,1024]{1,0:T(8,128)S(1)}, bf16[1024,1024]{1,0:T(8,128)(2,1)S(1)}) custom-call(bf16[1024,1024]{1,0:T(8,128)(2,1)S(1)} %shard_map.68.slope, bf16[16,1024]{1,0:T(8,128)(2,1)S(1)} %broadcast_in_dim.44.weights, bf16[16,1024]{1,0:T(8,128)(2,1)S(1)} %broadcast_in_dim.47.means, ...), custom_call_target="tpu_custom_call", output_to_operand_aliasing={{2}: (0, {})} | custom-call | flops 1 | bytes 1 | tf_op jit(solution)/shard_map/pallas_call | solution.py:371
  263.5 7.4 %shard_map.73 = bf16[768,1024]{1,0:T(8,128)(2,1)} custom-call(bf16[768,2048]{1,0:T(8,128)(2,1)} %copy-done, bf16[768,2048]{1,0:T(8,128)(2,1)} %copy-done.2, bf16[1024,1024]{1,0:T(8,128)(2,1)S(1)} %copy-done.8, bf16[1024,1024]{1,0:T(8,128)(2,1)S(1)} %copy-done.10, f32[768,1024]{1,0:T(8,128)} %shard_map.67.part, bf16[768,1024]{1,0:T(8,128)(2,1)S(1)} %copy-done.12, ...), custom_call_target="tpu_custom_call" | custom-call | flops 1 | bytes 1 | tf_op jit(solution)/shard_map/pallas_call | solution.py:246
  274.1 6.6 %shard_map.74 = bf16[768,1024]{1,0:T(8,128)(2,1)} custom-call(bf16[768,1024]{1,0:T(8,128)(2,1)S(1)} %copy-done.6, bf16[1024,1024]{1,0:T(8,128)(2,1)} %copy-done.7, bf16[768,1024]{1,0:T(8,128)(2,1)} %collective-permute-done.47.near, bf16[768,1024]{1,0:T(8,128)(2,1)} %collective-permute-done.44.across, bf16[768,1024]{1,0:T(8,128)(2,1)} %view.3, ...), custom_call_target="tpu_custom_call" | custom-call | flops 1 | bytes 1 | tf_op jit(solution)/shard_map/pallas_call | solution.py:287
  (209 shorter events, 136.6 us)
Async XLA Ops:
  0.7 36.4 %collective-permute-start = (bf16[768,1024]{1,0:T(8,128)(2,1)}, bf16[768,1024]{1,0:T(8,128)(2,1)}, u32[]{:S(2)}, u32[]{:S(2)}) collective-permute-start(bf16[768,1024]{1,0:T(8,128)(2,1)} %view.3), channel_id=1, source_target_pairs={{0,2},{1,3},{2,0},{3,1},{4,6},{5,7},{6,4},{7,5},{8,10},{9,11},{10,... | collective-permute-start | bytes 4718600 | tf_op jit(solution)/shard_map/ppermute | solution.py:41
  2.3 34.7 %collective-permute-start.1 = (bf16[768,1024]{1,0:T(8,128)(2,1)}, bf16[768,1024]{1,0:T(8,128)(2,1)}, u32[]{:S(2)}, u32[]{:S(2)}) collective-permute-start(bf16[768,1024]{1,0:T(8,128)(2,1)} %view.3), channel_id=1, source_target_pairs={{0,1},{1,0},{2,3},{3,2},{4,5},{5,4},{6,7},{7,6},{8,9},{9,8},{10,11... | collective-permute-start | bytes 4718600 | tf_op jit(solution)/shard_map/ppermute | solution.py:41
  61.0 17.3 %collective-permute-start.10 = (bf16[128,2048]{1,0:T(8,128)(2,1)}, bf16[128,2048]{1,0:T(8,128)(2,1)S(1)}, u32[]{:S(2)}, u32[]{:S(2)}) collective-permute-start(bf16[128,2048]{1,0:T(8,128)(2,1)} %get-tuple-element.153), channel_id=1, source_target_pairs={{0,48},{4,52},{8,56},{12,60},{16,0},{20,4},{24,8},{28,12},{32,16},... | collective-permute-start | bytes 1572872 | tf_op jit(solution)/shard_map/ppermute | solution.py:41
  64.1 16.6 %collective-permute-start.7 = (bf16[128,2048]{1,0:T(8,128)(2,1)}, bf16[128,2048]{1,0:T(8,128)(2,1)S(1)}, u32[]{:S(2)}, u32[]{:S(2)}) collective-permute-start(bf16[128,2048]{1,0:T(8,128)(2,1)} %get-tuple-element.150), channel_id=1, source_target_pairs={{0,4},{4,8},{8,12},{12,0},{16,20},{20,24},{24,28},{28,16},{32,36},... | collective-permute-start | bytes 1572872 | tf_op jit(solution)/shard_map/ppermute | solution.py:41
  66.0 14.6 %collective-permute-start.8 = (bf16[128,2048]{1,0:T(8,128)(2,1)}, bf16[128,2048]{1,0:T(8,128)(2,1)S(1)}, u32[]{:S(2)}, u32[]{:S(2)}) collective-permute-start(bf16[128,2048]{1,0:T(8,128)(2,1)} %get-tuple-element.151), channel_id=1, source_target_pairs={{0,12},{4,0},{8,4},{12,8},{16,28},{20,16},{24,20},{28,24},{32,44},... | collective-permute-start | bytes 1572872 | tf_op jit(solution)/shard_map/ppermute | solution.py:41
  68.1 15.3 %collective-permute-start.9 = (bf16[128,2048]{1,0:T(8,128)(2,1)}, bf16[128,2048]{1,0:T(8,128)(2,1)}, u32[]{:S(2)}, u32[]{:S(2)}) collective-permute-start(bf16[128,2048]{1,0:T(8,128)(2,1)} %get-tuple-element.152), channel_id=1, source_target_pairs={{0,16},{4,20},{8,24},{12,28},{16,32},{20,36},{24,40},{28,44},{32,4... | collective-permute-start | bytes 1572872 | tf_op jit(solution)/shard_map/ppermute | solution.py:41
  87.5 31.3 %collective-permute-start.11 = (bf16[256,2048]{1,0:T(8,128)(2,1)}, bf16[256,2048]{1,0:T(8,128)(2,1)}, u32[]{:S(2)}, u32[]{:S(2)}) collective-permute-start(bf16[256,2048]{1,0:T(8,128)(2,1)} %get-tuple-element.158), channel_id=1, source_target_pairs={{0,4},{4,8},{8,12},{12,0},{16,20},{20,24},{24,28},{28,16},{32,36},... | collective-permute-start | bytes 3145736 | tf_op jit(solution)/shard_map/ppermute | solution.py:41
  87.6 31.2 %collective-permute-start.12 = (bf16[256,2048]{1,0:T(8,128)(2,1)}, bf16[256,2048]{1,0:T(8,128)(2,1)}, u32[]{:S(2)}, u32[]{:S(2)}) collective-permute-start(bf16[256,2048]{1,0:T(8,128)(2,1)} %get-tuple-element.159), channel_id=1, source_target_pairs={{0,12},{4,0},{8,4},{12,8},{16,28},{20,16},{24,20},{28,24},{32,44},... | collective-permute-start | bytes 3145736 | tf_op jit(solution)/shard_map/ppermute | solution.py:41
  90.8 28.0 %collective-permute-start.13 = (bf16[256,2048]{1,0:T(8,128)(2,1)}, bf16[256,2048]{1,0:T(8,128)(2,1)}, u32[]{:S(2)}, u32[]{:S(2)}) collective-permute-start(bf16[256,2048]{1,0:T(8,128)(2,1)} %get-tuple-element.160), channel_id=1, source_target_pairs={{0,16},{4,20},{8,24},{12,28},{16,32},{20,36},{24,40},{28,44},{32,4... | collective-permute-start | bytes 3145736 | tf_op jit(solution)/shard_map/ppermute | solution.py:41
  90.8 28.0 %collective-permute-start.14 = (bf16[256,2048]{1,0:T(8,128)(2,1)}, bf16[256,2048]{1,0:T(8,128)(2,1)}, u32[]{:S(2)}, u32[]{:S(2)}) collective-permute-start(bf16[256,2048]{1,0:T(8,128)(2,1)} %get-tuple-element.161), channel_id=1, source_target_pairs={{0,48},{4,52},{8,56},{12,60},{16,0},{20,4},{24,8},{28,12},{32,16},... | collective-permute-start | bytes 3145736 | tf_op jit(solution)/shard_map/ppermute | solution.py:41
  99.6 19.2 %all-to-all-start.1 = ((f32[16,40,128]{2,1,0:T(8,128)}), f32[16,40,128]{2,1,0:T(8,128)S(1)}, u32[]{:S(2)}, u32[]{:S(2)}) async-start(f32[16,40,128]{2,1,0:T(8,128)} %broadcast_in_dim.43), calls=%async_computation.1 | async-start | bytes 655360 | tf_op jit(solution)/shard_map/all_to_all | solution.py:52
  171.8 15.8 %collective-permute-start.29 = (bf16[256,1024]{1,0:T(8,128)(2,1)S(1)}, bf16[256,1024]{1,0:T(8,128)(2,1)S(1)}, u32[]{:S(2)}, u32[]{:S(2)}) collective-permute-start(bf16[256,1024]{1,0:T(8,128)(2,1)S(1)} %get-tuple-element.206.refs_0_), channel_id=1, source_target_pairs={{0,8},{4,12},{8,0},{12,4},{16,24},{20,28},{24,16},{28,20},{32,40},... | collective-permute-start | bytes 1572872 | tf_op jit(solution)/shard_map/ppermute | solution.py:41
  172.9 20.1 %collective-permute-start.30 = (bf16[256,1024]{1,0:T(8,128)(2,1)S(1)}, bf16[256,1024]{1,0:T(8,128)(2,1)S(1)}, u32[]{:S(2)}, u32[]{:S(2)}) collective-permute-start(bf16[256,1024]{1,0:T(8,128)(2,1)S(1)} %get-tuple-element.206.refs_0_), channel_id=1, source_target_pairs={{0,4},{4,8},{8,12},{12,0},{16,20},{20,24},{24,28},{28,16},{32,36},... | collective-permute-start | bytes 1572872 | tf_op jit(solution)/shard_map/ppermute | solution.py:41
  175.6 18.4 %collective-permute-start.31 = (bf16[256,1024]{1,0:T(8,128)(2,1)S(1)}, bf16[256,1024]{1,0:T(8,128)(2,1)S(1)}, u32[]{:S(2)}, u32[]{:S(2)}) collective-permute-start(bf16[256,1024]{1,0:T(8,128)(2,1)S(1)} %get-tuple-element.206.refs_0_), channel_id=1, source_target_pairs={{0,12},{4,0},{8,4},{12,8},{16,28},{20,16},{24,20},{28,24},{32,44},... | collective-permute-start | bytes 1572872 | tf_op jit(solution)/shard_map/ppermute | solution.py:41
  176.2 17.8 %collective-permute-start.32 = (bf16[256,1024]{1,0:T(8,128)(2,1)S(1)}, bf16[256,1024]{1,0:T(8,128)(2,1)S(1)}, u32[]{:S(2)}, u32[]{:S(2)}) collective-permute-start(bf16[256,1024]{1,0:T(8,128)(2,1)S(1)} %get-tuple-element.209.refs_0_), channel_id=1, source_target_pairs={{0,32},{4,36},{8,40},{12,44},{16,48},{20,52},{24,56},{28,60},{32,0... | collective-permute-start | bytes 1572872 | tf_op jit(solution)/shard_map/ppermute | solution.py:41
  208.4 46.1 %collective-permute-start.44 = (bf16[768,1024]{1,0:T(8,128)(2,1)}, bf16[768,1024]{1,0:T(8,128)(2,1)}, u32[]{:S(2)}, u32[]{:S(2)}) collective-permute-start(bf16[768,1024]{1,0:T(8,128)(2,1)} %add_convert_fusion), channel_id=1, source_target_pairs={{0,2},{1,3},{2,0},{3,1},{4,6},{5,7},{6,4},{7,5},{8,10},{9,11},{10,... | collective-permute-start | bytes 4718600 | tf_op jit(solution)/shard_map/ppermute | solution.py:41
  208.7 15.3 %collective-permute-start.36 = (bf16[256,1024]{1,0:T(8,128)(2,1)S(1)}, bf16[256,1024]{1,0:T(8,128)(2,1)S(1)}, u32[]{:S(2)}, u32[]{:S(2)}) collective-permute-start(bf16[256,1024]{1,0:T(8,128)(2,1)S(1)} %get-tuple-element.219.refs_0_), channel_id=1, source_target_pairs={{0,4},{4,8},{8,12},{12,0},{16,20},{20,24},{24,28},{28,16},{32,36},... | collective-permute-start | bytes 1572872 | tf_op jit(solution)/shard_map/ppermute | solution.py:41
  210.7 13.8 %collective-permute-start.37 = (bf16[256,1024]{1,0:T(8,128)(2,1)S(1)}, bf16[256,1024]{1,0:T(8,128)(2,1)S(1)}, u32[]{:S(2)}, u32[]{:S(2)}) collective-permute-start(bf16[256,1024]{1,0:T(8,128)(2,1)S(1)} %get-tuple-element.219.refs_0_), channel_id=1, source_target_pairs={{0,12},{4,0},{8,4},{12,8},{16,28},{20,16},{24,20},{28,24},{32,44},... | collective-permute-start | bytes 1572872 | tf_op jit(solution)/shard_map/ppermute | solution.py:41
  211.9 15.5 %collective-permute-start.38 = (bf16[256,1024]{1,0:T(8,128)(2,1)S(1)}, bf16[256,1024]{1,0:T(8,128)(2,1)S(1)}, u32[]{:S(2)}, u32[]{:S(2)}) collective-permute-start(bf16[256,1024]{1,0:T(8,128)(2,1)S(1)} %get-tuple-element.221.refs_0_), channel_id=1, source_target_pairs={{0,16},{4,20},{8,24},{12,28},{16,32},{20,36},{24,40},{28,44},{32,4... | collective-permute-start | bytes 1572872 | tf_op jit(solution)/shard_map/ppermute | solution.py:41
  212.0 15.4 %collective-permute-start.39 = (bf16[256,1024]{1,0:T(8,128)(2,1)S(1)}, bf16[256,1024]{1,0:T(8,128)(2,1)S(1)}, u32[]{:S(2)}, u32[]{:S(2)}) collective-permute-start(bf16[256,1024]{1,0:T(8,128)(2,1)S(1)} %get-tuple-element.221.refs_0_), channel_id=1, source_target_pairs={{0,48},{4,52},{8,56},{12,60},{16,0},{20,4},{24,8},{28,12},{32,16},... | collective-permute-start | bytes 1572872 | tf_op jit(solution)/shard_map/ppermute | solution.py:41
  227.7 13.5 %collective-permute-start.40 = (bf16[128,1024]{1,0:T(8,128)(2,1)S(1)}, bf16[128,1024]{1,0:T(8,128)(2,1)S(1)}, u32[]{:S(2)}, u32[]{:S(2)}) collective-permute-start(bf16[128,1024]{1,0:T(8,128)(2,1)S(1)} %get-tuple-element.231), channel_id=1, source_target_pairs={{0,4},{4,8},{8,12},{12,0},{16,20},{20,24},{24,28},{28,16},{32,36},... | collective-permute-start | bytes 786440 | tf_op jit(solution)/shard_map/ppermute | solution.py:41
  227.8 13.4 %collective-permute-start.41 = (bf16[128,1024]{1,0:T(8,128)(2,1)S(1)}, bf16[128,1024]{1,0:T(8,128)(2,1)S(1)}, u32[]{:S(2)}, u32[]{:S(2)}) collective-permute-start(bf16[128,1024]{1,0:T(8,128)(2,1)S(1)} %get-tuple-element.232), channel_id=1, source_target_pairs={{0,12},{4,0},{8,4},{12,8},{16,28},{20,16},{24,20},{28,24},{32,44},... | collective-permute-start | bytes 786440 | tf_op jit(solution)/shard_map/ppermute | solution.py:41
  254.6 19.5 %collective-permute-start.47 = (bf16[768,1024]{1,0:T(8,128)(2,1)}, bf16[768,1024]{1,0:T(8,128)(2,1)}, u32[]{:S(2)}, u32[]{:S(2)}) collective-permute-start(bf16[768,1024]{1,0:T(8,128)(2,1)} %copy-done.15), channel_id=1, source_target_pairs={{0,1},{1,0},{2,3},{3,2},{4,5},{5,4},{6,7},{7,6},{8,9},{9,8},{10,11... | collective-permute-start | bytes 4718600 | tf_op jit(solution)/shard_map/ppermute | solution.py:41
  258.5 14.4 %collective-permute-start.46 = (f32[3,1024]{1,0:T(4,128)S(1)}, f32[3,1024]{1,0:T(4,128)S(1)}, u32[]{:S(2)}, u32[]{:S(2)}) collective-permute-start(f32[3,1024]{1,0:T(4,128)S(1)} %pad_maximum_fusion.5), channel_id=1, source_target_pairs={{0,2},{1,3},{2,0},{3,1},{4,6},{5,7},{6,4},{7,5},{8,10},{9,11},{10,... | collective-permute-start | bytes 36872 | tf_op jit(solution)/shard_map/ppermute | solution.py:41
  (43 other events, 334.2 us)

commit v2 on v1

--- a/solution.py
+++ b/solution.py
@@ -574,23 +574,22 @@
     near = times(low_a, slope_e, low)
     columns_b, rows_b, slope_b = slope_terms(slope_b, weights, means[0], wide_slope)
     columns_e, rows_e = slope_terms(slope_e, weights, means[2])
-    loss = jnp.sum(columns_b[2].reshape(16, 64)[:, :3])
-    loss_row = jnp.full((1, width), loss)
-    small = jnp.concatenate((columns_e[:2], columns_d[:2], loss_row))
+    small = jnp.concatenate((columns_e[:2], columns_d[:2]))
     across, near, small = lax.optimization_barrier((across, near, small))
     diagonal_term = diagonal_slope * diagonal
     near, small = stage([(near, core), (small, core)])
-    distant = stage([(jnp.concatenate((columns_c[:2] + small[2:4], loss_row + small[4:5])), chip)])[0]
+    slots = columns_b[2:3]
+    distant = stage([(jnp.concatenate((columns_c[:2] + small[2:4], slots)), chip)])[0]
     rows_a = rows_b[:2] + rows_c[:2] + rows_d[:2] + rows_e[:2]
     rows_a = jnp.concatenate(((rows_a[0] + diagonal_term)[None], rows_a[1:2]))
     stats_a = jnp.concatenate((mean[0:1], inv_a[None], rows_a, jnp.zeros((4, width), full)))
     grad_a = up_a_call(0, low_even, low_odd, slope_b, slope_e, part_a, view_a, stats_a)
     grad_a, distant = lax.optimization_barrier((grad_a, distant))
-    loss = loss + small[4, 0] + distant[2, 0]
-    zeros = jnp.zeros((4, width), full)
+    slots = slots + distant[2:3]
+    loss = jnp.sum(slots + stage([(slots, core)])[0])
     columns = columns_b[:2] + small[0:2] + distant[0:2]
     columns = jnp.concatenate(((columns[0] + diagonal_term)[None], columns[1:2]))
-    stats_b = jnp.concatenate((mean[1:2], inv_b[None], columns, zeros))
+    stats_b = jnp.concatenate((mean[1:2], inv_b[None], columns, jnp.zeros((4, width), full)))
     grad_b = grad_b_call(low_a, slope_b, near, across, view_b, stats_b)
     return (loss, grad_a, grad_b)
 

time: 284 us -> 279 us (0.982)
  between operations: 4.38 us -> 1.29 us
    unnamed x36 -> x38, local copies, waits for them, and re-layouts: 9.63 us -> 11 us
    ppermute x48 -> x49, waiting for transfers between devices: 58.4 us -> 57.8 us  [stage(): lax.ppermute(values, axis, [(d, place(d)) for d in range(count)])]
    ppermute x48 -> x49, starting transfers between devices: 80 us -> 79.6 us  [stage(): lax.ppermute(values, axis, [(d, place(d)) for d in range(count)])]
  transfers between devices with their start and end apart: 49 -> 50, of which waited for: 23 -> 24; matrix products, arithmetic and copies ran while one was open for 5% -> 5% of each run, Pallas kernels for 17% -> 18%
where the time goes in v2:
time: 279 us; the launch traced here: 277 us
  starting transfers between devices  83.1 us (30%)
  Pallas kernels  74.7 us (27%)
  waiting for transfers between devices  70.1 us (25%)
  blocking collectives  17.7 us (6%)
  local copies, waits for them, and re-layouts  12.3 us (4%)
  other arithmetic  11.9 us (4%)
  matrix products  5.72 us (2%)
    ppermute x49, starting transfers between devices, stage(): lax.ppermute(values, axis, [(d, place(d)) for d in range(count)])  79.6 us
    ppermute x49, waiting for transfers between devices, stage(): lax.ppermute(values, axis, [(d, place(d)) for d in range(count)])  57.8 us
    all_to_all x1, blocking collectives, share(): lax.all_to_all(pieces, 'dp', 0, 0, tiled=True, axis_index_groups=groups)  17.7 us
    pallas_call x2, Pallas kernels, up_a_call(): pl.pallas_call(grad_kernel if more else part_kernel, grid=(width // 256,)...  14.4 us
    all_to_all x1, waiting for transfers between devices, share(): lax.all_to_all(pieces, 'dp', 0, 0, tiled=True, axis_index_groups=groups)  12.3 us
    pallas_call x4, Pallas kernels, slope_terms(): pl.pallas_call(terms_kernel, grid=(4,), in_specs=[tile, pl.BlockSpec((16,...  12.3 us
    unnamed x38, local copies, waits for them, and re-layouts  11 us
    pallas_call x2, Pallas kernels, near_chunks(): pl.pallas_call(near_kernel, grid_spec=pltpu.PrefetchScalarGridSpec(num_sc...  10.1 us
  transfers between devices with their start and end apart: 50, of which 24 were waited for; matrix products, arithmetic and copies ran while one was open for 5% of the time, Pallas kernels for 18%

profile of v2, /device:TPU:0, one launch (start us, length us, event | category | flops | bytes accessed | tf_op | source)
XLA Modules:
  0.0 276.8 jit_solution(1891943998621265378)
XLA Ops:
  5.5 17.7 %all_to_all.10 = f32[16,40,128]{2,1,0:T(8,128)S(1)} all-to-all(f32[16,40,128]{2,1,0:T(8,128)S(1)} %broadcast_in_dim.38), channel_id=1, replica_groups={{0,4,8,12,16,20,24,28,32,36,40,44,48,52,56,60},{64,68,72,76,80,84,88,92..., dimensions={0} | all-to-all | bytes 655360 | tf_op jit(solution)/shard_map/all_to_all | solution.py:52
  23.7 13.3 %collective-permute-done.view_c = bf16[768,1024]{1,0:T(8,128)(2,1)} collective-permute-done((bf16[768,1024]{1,0:T(8,128)(2,1)}, bf16[768,1024]{1,0:T(8,128)(2,1)}, u32[]{:S(2)}, u32[]{:S(2)}) %collective-permute-start) | collective-permute-done | bytes 1572896 | tf_op jit(solution)/shard_map/ppermute | solution.py:41
  37.0 3.3 %collective-permute-start.2 = (f32[5,1024]{1,0:T(8,128)S(1)}, f32[5,1024]{1,0:T(8,128)S(1)}, u32[]{:S(2)}, u32[]{:S(2)}) collective-permute-start(f32[5,1024]{1,0:T(8,128)S(1)} %pad_maximum_fusion.2), channel_id=1, source_target_pairs={{0,64},{4,68},{8,72},{12,76},{16,80},{20,84},{24,88},{28,92},{32,9... | collective-permute-start | bytes 61448 | tf_op jit(solution)/shard_map/ppermute | solution.py:41
  57.7 3.3 %shard_map.54 = (bf16[128,2048]{1,0:T(8,128)(2,1)}, bf16[128,2048]{1,0:T(8,128)(2,1)}) custom-call(s32[1]{0:T(128)} %bitcast.14.position, bf16[768,1024]{1,0:T(8,128)(2,1)S(1)} %get-tuple-element.261.left, bf16[768,2048]{1,0:T(8,128)(2,1)S(1)} %shard_map.50.right.odd), custom_call_target="tpu_custom_call" | custom-call | tf_op jit(solution)/shard_map/pallas_call | solution.py:192
  68.2 5.1 %shard_map.51 = (bf16[256,2048]{1,0:T(8,128)(2,1)}, bf16[256,2048]{1,0:T(8,128)(2,1)}) custom-call(s32[1]{0:T(128)} %bitcast.position, bf16[768,1024]{1,0:T(8,128)(2,1)S(1)} %get-tuple-element.261.left, bf16[768,2048]{1,0:T(8,128)(2,1)} %copy-done), custom_call_target="tpu_custom_call" | custom-call | tf_op jit(solution)/shard_map/pallas_call | solution.py:176
  73.2 5.1 %shard_map.52 = (bf16[256,2048]{1,0:T(8,128)(2,1)}, bf16[256,2048]{1,0:T(8,128)(2,1)}) custom-call(s32[1]{0:T(128)} %bitcast.10.position, bf16[768,1024]{1,0:T(8,128)(2,1)S(1)} %get-tuple-element.261.left, bf16[768,2048]{1,0:T(8,128)(2,1)} %copy-done.2), custom_call_target="tpu_custom_call" | custom-call | tf_op jit(solution)/shard_map/pallas_call | solution.py:176
  83.4 4.1 %shard_map.55 = (bf16[256,2048]{1,0:T(8,128)(2,1)}, bf16[256,2048]{1,0:T(8,128)(2,1)}, bf16[256,2048]{1,0:T(8,128)(2,1)}, bf16[256,2048]{1,0:T(8,128)(2,1)}) custom-call(bf16[256,2048]{1,0:T(8,128)(2,1)} %get-tuple-element.142.refs_0_, ...), custom_call_target="tpu_custom_call", output_to_operand_aliasing={{0}: (0, {}), {1}: (1, {}), {2}: (2, {}), {3}: (3, {})} | custom-call | tf_op jit(solution)/shard_map/pallas_call | solution.py:97
  87.6 3.2 %collective-permute-start.12 = (bf16[256,2048]{1,0:T(8,128)(2,1)}, bf16[256,2048]{1,0:T(8,128)(2,1)}, u32[]{:S(2)}, u32[]{:S(2)}) collective-permute-start(bf16[256,2048]{1,0:T(8,128)(2,1)} %get-tuple-element.159), channel_id=1, source_target_pairs={{0,12},{4,0},{8,4},{12,8},{16,28},{20,16},{24,20},{28,24},{32,44},... | collective-permute-start | bytes 3145736 | tf_op jit(solution)/shard_map/ppermute | solution.py:41
  90.8 3.2 %collective-permute-start.14 = (bf16[256,2048]{1,0:T(8,128)(2,1)}, bf16[256,2048]{1,0:T(8,128)(2,1)}, u32[]{:S(2)}, u32[]{:S(2)}) collective-permute-start(bf16[256,2048]{1,0:T(8,128)(2,1)} %get-tuple-element.161), channel_id=1, source_target_pairs={{0,48},{4,52},{8,56},{12,60},{16,0},{20,4},{24,8},{28,12},{32,16},... | collective-permute-start | bytes 3145736 | tf_op jit(solution)/shard_map/ppermute | solution.py:41
  99.6 3.5 %all-to-all-start.1 = ((f32[16,40,128]{2,1,0:T(8,128)}), f32[16,40,128]{2,1,0:T(8,128)S(1)}, u32[]{:S(2)}, u32[]{:S(2)}) async-start(f32[16,40,128]{2,1,0:T(8,128)} %broadcast_in_dim.40), calls=%async_computation.1 | async-start | bytes 655360 | tf_op jit(solution)/shard_map/all_to_all | solution.py:52
  103.1 3.3 %fusion.8.refs_3_ = f32[256,2048]{1,0:T(8,128)} fusion(bf16[768,2048]{1,0:T(8,128)(2,1)S(1)} %copy-done.4, bf16[768,1024]{1,0:T(8,128)(2,1)} %copy-done.5, s32[]{:T(128)S(6)} %select_n.7), kind=kOutput, calls=%fused_computation.20 | convolution fusion | flops 805306368 | bytes 5636100 | tf_op jit(solution)/shard_map/dot_general | solution.py:492
  106.5 12.3 %all-to-all-done.1 = f32[16,40,128]{2,1,0:T(8,128)S(1)} async-done(((f32[16,40,128]{2,1,0:T(8,128)}), f32[16,40,128]{2,1,0:T(8,128)S(1)}, u32[]{:S(2)}, u32[]{:S(2)}) %all-to-all-start.1) | async-done | bytes 327712 | tf_op jit(solution)/shard_map/all_to_all | solution.py:52
  118.8 5.0 %shard_map.56 = (f32[64,2048]{1,0:T(8,128)S(1)}, bf16[64,2048]{1,0:T(8,128)(2,1)S(1)}, bf16[64,2048]{1,0:T(8,128)(2,1)S(1)}, bf16[64,2048]{1,0:T(8,128)(2,1)S(1)...) custom-call(s32[2]{0:T(128)S(1)} %pad_add_fusion.places, ...), custom_call_target="tpu_custom_call" | custom-call | tf_op jit(solution)/shard_map/pallas_call | solution.py:319
  133.2 3.4 %collective-permute-start.20 = (bf16[64,2048]{1,0:T(8,128)(2,1)S(1)}, bf16[64,2048]{1,0:T(8,128)(2,1)S(1)}, u32[]{:S(2)}, u32[]{:S(2)}) collective-permute-start(bf16[64,2048]{1,0:T(8,128)(2,1)S(1)} %get-tuple-element.180), channel_id=1, source_target_pairs={{0,12},{4,0},{8,4},{12,8},{16,28},{20,16},{24,20},{28,24},{32,44},... | collective-permute-start | bytes 786440 | tf_op jit(solution)/shard_map/ppermute | solution.py:41
  146.4 8.6 %collective-permute-done.22 = f32[40,128]{1,0:T(8,128)S(1)} collective-permute-done((f32[40,128]{1,0:T(8,128)S(1)}, f32[40,128]{1,0:T(8,128)S(1)}, u32[]{:S(2)}, u32[]{:S(2)}) %collective-permute-start.22) | collective-permute-done | bytes 20512 | tf_op jit(solution)/shard_map/ppermute | solution.py:41
  176.2 7.5 %collective-permute-start.32 = (bf16[256,1024]{1,0:T(8,128)(2,1)S(1)}, bf16[256,1024]{1,0:T(8,128)(2,1)S(1)}, u32[]{:S(2)}, u32[]{:S(2)}) collective-permute-start(bf16[256,1024]{1,0:T(8,128)(2,1)S(1)} %get-tuple-element.209.refs_0_), channel_id=1, source_target_pairs={{0,32},{4,36},{8,40},{12,44},{16,48},{20,52},{24,56},{28,60},{32,0... | collective-permute-start | bytes 1572872 | tf_op jit(solution)/shard_map/ppermute | solution.py:41
  187.5 3.5 %collective-permute-start.34 = (bf16[256,1024]{1,0:T(8,128)(2,1)S(1)}, bf16[256,1024]{1,0:T(8,128)(2,1)S(1)}, u32[]{:S(2)}, u32[]{:S(2)}) collective-permute-start(bf16[256,1024]{1,0:T(8,128)(2,1)S(1)} %get-tuple-element.209.refs_0_), channel_id=1, source_target_pairs={{0,48},{4,52},{8,56},{12,60},{16,0},{20,4},{24,8},{28,12},{32,16},... | collective-permute-start | bytes 1572872 | tf_op jit(solution)/shard_map/ppermute | solution.py:41
  201.2 3.4 %shard_map.61 = f32[768,1024]{1,0:T(8,128)} custom-call(bf16[768,1024]{1,0:T(8,128)(2,1)S(1)} %copy-done.6, bf16[1024,1024]{1,0:T(8,128)(2,1)S(1)} %shard_map.60.right.slope.slope_even), custom_call_target="tpu_custom_call" | custom-call | flops 1 | bytes 1 | tf_op jit(solution)/shard_map/pallas_call | solution.py:212
  204.6 3.6 %add_convert_fusion = bf16[768,1024]{1,0:T(8,128)(2,1)} fusion(f32[768,1024]{1,0:T(8,128)} %shard_map.61, bf16[768,1024]{1,0:T(8,128)(2,1)S(1)} %collective-permute-done.35), kind=kLoop, calls=%fused_computation.15 | loop fusion | flops 2359296 | bytes 6291456 | tf_op jit(solution)/shard_map/convert_element_type | solution.py:557
  212.0 3.3 %collective-permute-start.39 = (bf16[256,1024]{1,0:T(8,128)(2,1)S(1)}, bf16[256,1024]{1,0:T(8,128)(2,1)S(1)}, u32[]{:S(2)}, u32[]{:S(2)}) collective-permute-start(bf16[256,1024]{1,0:T(8,128)(2,1)S(1)} %get-tuple-element.221.refs_0_), channel_id=1, source_target_pairs={{0,48},{4,52},{8,56},{12,60},{16,0},{20,4},{24,8},{28,12},{32,16},... | collective-permute-start | bytes 1572872 | tf_op jit(solution)/shard_map/ppermute | solution.py:41
  234.1 7.0 %shard_map.67.part = f32[768,1024]{1,0:T(8,128)} custom-call(bf16[768,2048]{1,0:T(8,128)(2,1)} %copy-done, bf16[768,2048]{1,0:T(8,128)(2,1)} %copy-done.2, bf16[1024,1024]{1,0:T(8,128)(2,1)S(1)} %shard_map.60.right.slope.slope_even, bf16[1024,1024]{1,0:T(8,128)(2,1)S(1)} %shard_map.62.right.slope.slope_odd), custom_call_target="tpu_custom_call" | custom-call | flops 1 | bytes 1 | tf_op jit(solution)/shard_map/pallas_call | solution.py:246
  247.5 4.0 %shard_map.69 = (f32[8,1024]{1,0:T(8,128)S(1)}, f32[8,1024]{1,0:T(8,128)S(1)}, bf16[1024,1024]{1,0:T(8,128)(2,1)S(1)}) custom-call(bf16[1024,1024]{1,0:T(8,128)(2,1)S(1)} %shard_map.68.slope, bf16[16,1024]{1,0:T(8,128)(2,1)S(1)} %broadcast_in_dim.41.weights, bf16[16,1024]{1,0:T(8,128)(2,1)S(1)} %broadcast_in_dim.44.means, ...), custom_call_target="tpu_custom_call", output_to_operand_aliasing={{2}: (0, {})} | custom-call | flops 1 | bytes 1 | tf_op jit(solution)/shard_map/pallas_call | solution.py:371
  260.2 7.4 %shard_map.72 = bf16[768,1024]{1,0:T(8,128)(2,1)} custom-call(bf16[768,2048]{1,0:T(8,128)(2,1)} %copy-done, bf16[768,2048]{1,0:T(8,128)(2,1)} %copy-done.2, bf16[1024,1024]{1,0:T(8,128)(2,1)S(1)} %copy-done.8, bf16[1024,1024]{1,0:T(8,128)(2,1)S(1)} %copy-done.10, f32[768,1024]{1,0:T(8,128)} %shard_map.67.part, bf16[768,1024]{1,0:T(8,128)(2,1)S(1)} %copy-done.12, ...), custom_call_target="tpu_custom_call" | custom-call | flops 1 | bytes 1 | tf_op jit(solution)/shard_map/pallas_call | solution.py:246
  270.9 5.9 %shard_map.74 = bf16[768,1024]{1,0:T(8,128)(2,1)} custom-call(bf16[768,1024]{1,0:T(8,128)(2,1)S(1)} %copy-done.6, bf16[1024,1024]{1,0:T(8,128)(2,1)} %copy-done.7, bf16[768,1024]{1,0:T(8,128)(2,1)} %collective-permute-done.48.near, bf16[768,1024]{1,0:T(8,128)(2,1)S(1)} %copy-done.16, bf16[768,1024]{1,0:T(8,128)(2,1)} %view.3, f32[8,1024]{1,0:T(8,128)S(1)} %concatenate.31.stats), custom_call_target="tpu_custom_call" | custom-call | flops 1 | bytes 1 | tf_op jit(solution)/shard_map/pallas_call | solution.py:287
  (209 shorter events, 135.6 us)
Async XLA Ops:
  0.7 36.4 %collective-permute-start = (bf16[768,1024]{1,0:T(8,128)(2,1)}, bf16[768,1024]{1,0:T(8,128)(2,1)}, u32[]{:S(2)}, u32[]{:S(2)}) collective-permute-start(bf16[768,1024]{1,0:T(8,128)(2,1)} %view.3), channel_id=1, source_target_pairs={{0,2},{1,3},{2,0},{3,1},{4,6},{5,7},{6,4},{7,5},{8,10},{9,11},{10,... | collective-permute-start | bytes 4718600 | tf_op jit(solution)/shard_map/ppermute | solution.py:41
  2.3 34.7 %collective-permute-start.1 = (bf16[768,1024]{1,0:T(8,128)(2,1)}, bf16[768,1024]{1,0:T(8,128)(2,1)}, u32[]{:S(2)}, u32[]{:S(2)}) collective-permute-start(bf16[768,1024]{1,0:T(8,128)(2,1)} %view.3), channel_id=1, source_target_pairs={{0,1},{1,0},{2,3},{3,2},{4,5},{5,4},{6,7},{7,6},{8,9},{9,8},{10,11... | collective-permute-start | bytes 4718600 | tf_op jit(solution)/shard_map/ppermute | solution.py:41
  61.0 17.3 %collective-permute-start.10 = (bf16[128,2048]{1,0:T(8,128)(2,1)}, bf16[128,2048]{1,0:T(8,128)(2,1)S(1)}, u32[]{:S(2)}, u32[]{:S(2)}) collective-permute-start(bf16[128,2048]{1,0:T(8,128)(2,1)} %get-tuple-element.153), channel_id=1, source_target_pairs={{0,48},{4,52},{8,56},{12,60},{16,0},{20,4},{24,8},{28,12},{32,16},... | collective-permute-start | bytes 1572872 | tf_op jit(solution)/shard_map/ppermute | solution.py:41
  64.0 16.6 %collective-permute-start.7 = (bf16[128,2048]{1,0:T(8,128)(2,1)}, bf16[128,2048]{1,0:T(8,128)(2,1)S(1)}, u32[]{:S(2)}, u32[]{:S(2)}) collective-permute-start(bf16[128,2048]{1,0:T(8,128)(2,1)} %get-tuple-element.150), channel_id=1, source_target_pairs={{0,4},{4,8},{8,12},{12,0},{16,20},{20,24},{24,28},{28,16},{32,36},... | collective-permute-start | bytes 1572872 | tf_op jit(solution)/shard_map/ppermute | solution.py:41
  66.0 14.6 %collective-permute-start.8 = (bf16[128,2048]{1,0:T(8,128)(2,1)}, bf16[128,2048]{1,0:T(8,128)(2,1)S(1)}, u32[]{:S(2)}, u32[]{:S(2)}) collective-permute-start(bf16[128,2048]{1,0:T(8,128)(2,1)} %get-tuple-element.151), channel_id=1, source_target_pairs={{0,12},{4,0},{8,4},{12,8},{16,28},{20,16},{24,20},{28,24},{32,44},... | collective-permute-start | bytes 1572872 | tf_op jit(solution)/shard_map/ppermute | solution.py:41
  68.1 15.3 %collective-permute-start.9 = (bf16[128,2048]{1,0:T(8,128)(2,1)}, bf16[128,2048]{1,0:T(8,128)(2,1)}, u32[]{:S(2)}, u32[]{:S(2)}) collective-permute-start(bf16[128,2048]{1,0:T(8,128)(2,1)} %get-tuple-element.152), channel_id=1, source_target_pairs={{0,16},{4,20},{8,24},{12,28},{16,32},{20,36},{24,40},{28,44},{32,4... | collective-permute-start | bytes 1572872 | tf_op jit(solution)/shard_map/ppermute | solution.py:41
  87.5 31.3 %collective-permute-start.11 = (bf16[256,2048]{1,0:T(8,128)(2,1)}, bf16[256,2048]{1,0:T(8,128)(2,1)}, u32[]{:S(2)}, u32[]{:S(2)}) collective-permute-start(bf16[256,2048]{1,0:T(8,128)(2,1)} %get-tuple-element.158), channel_id=1, source_target_pairs={{0,4},{4,8},{8,12},{12,0},{16,20},{20,24},{24,28},{28,16},{32,36},... | collective-permute-start | bytes 3145736 | tf_op jit(solution)/shard_map/ppermute | solution.py:41
  87.6 31.2 %collective-permute-start.12 = (bf16[256,2048]{1,0:T(8,128)(2,1)}, bf16[256,2048]{1,0:T(8,128)(2,1)}, u32[]{:S(2)}, u32[]{:S(2)}) collective-permute-start(bf16[256,2048]{1,0:T(8,128)(2,1)} %get-tuple-element.159), channel_id=1, source_target_pairs={{0,12},{4,0},{8,4},{12,8},{16,28},{20,16},{24,20},{28,24},{32,44},... | collective-permute-start | bytes 3145736 | tf_op jit(solution)/shard_map/ppermute | solution.py:41
  90.8 28.0 %collective-permute-start.13 = (bf16[256,2048]{1,0:T(8,128)(2,1)}, bf16[256,2048]{1,0:T(8,128)(2,1)}, u32[]{:S(2)}, u32[]{:S(2)}) collective-permute-start(bf16[256,2048]{1,0:T(8,128)(2,1)} %get-tuple-element.160), channel_id=1, source_target_pairs={{0,16},{4,20},{8,24},{12,28},{16,32},{20,36},{24,40},{28,44},{32,4... | collective-permute-start | bytes 3145736 | tf_op jit(solution)/shard_map/ppermute | solution.py:41
  90.8 28.0 %collective-permute-start.14 = (bf16[256,2048]{1,0:T(8,128)(2,1)}, bf16[256,2048]{1,0:T(8,128)(2,1)}, u32[]{:S(2)}, u32[]{:S(2)}) collective-permute-start(bf16[256,2048]{1,0:T(8,128)(2,1)} %get-tuple-element.161), channel_id=1, source_target_pairs={{0,48},{4,52},{8,56},{12,60},{16,0},{20,4},{24,8},{28,12},{32,16},... | collective-permute-start | bytes 3145736 | tf_op jit(solution)/shard_map/ppermute | solution.py:41
  99.6 19.2 %all-to-all-start.1 = ((f32[16,40,128]{2,1,0:T(8,128)}), f32[16,40,128]{2,1,0:T(8,128)S(1)}, u32[]{:S(2)}, u32[]{:S(2)}) async-start(f32[16,40,128]{2,1,0:T(8,128)} %broadcast_in_dim.40), calls=%async_computation.1 | async-start | bytes 655360 | tf_op jit(solution)/shard_map/all_to_all | solution.py:52
  171.8 15.7 %collective-permute-start.29 = (bf16[256,1024]{1,0:T(8,128)(2,1)S(1)}, bf16[256,1024]{1,0:T(8,128)(2,1)S(1)}, u32[]{:S(2)}, u32[]{:S(2)}) collective-permute-start(bf16[256,1024]{1,0:T(8,128)(2,1)S(1)} %get-tuple-element.206.refs_0_), channel_id=1, source_target_pairs={{0,8},{4,12},{8,0},{12,4},{16,24},{20,28},{24,16},{28,20},{32,40},... | collective-permute-start | bytes 1572872 | tf_op jit(solution)/shard_map/ppermute | solution.py:41
  173.0 20.1 %collective-permute-start.30 = (bf16[256,1024]{1,0:T(8,128)(2,1)S(1)}, bf16[256,1024]{1,0:T(8,128)(2,1)S(1)}, u32[]{:S(2)}, u32[]{:S(2)}) collective-permute-start(bf16[256,1024]{1,0:T(8,128)(2,1)S(1)} %get-tuple-element.206.refs_0_), channel_id=1, source_target_pairs={{0,4},{4,8},{8,12},{12,0},{16,20},{20,24},{24,28},{28,16},{32,36},... | collective-permute-start | bytes 1572872 | tf_op jit(solution)/shard_map/ppermute | solution.py:41
  175.6 18.4 %collective-permute-start.31 = (bf16[256,1024]{1,0:T(8,128)(2,1)S(1)}, bf16[256,1024]{1,0:T(8,128)(2,1)S(1)}, u32[]{:S(2)}, u32[]{:S(2)}) collective-permute-start(bf16[256,1024]{1,0:T(8,128)(2,1)S(1)} %get-tuple-element.206.refs_0_), channel_id=1, source_target_pairs={{0,12},{4,0},{8,4},{12,8},{16,28},{20,16},{24,20},{28,24},{32,44},... | collective-permute-start | bytes 1572872 | tf_op jit(solution)/shard_map/ppermute | solution.py:41
  176.2 17.8 %collective-permute-start.32 = (bf16[256,1024]{1,0:T(8,128)(2,1)S(1)}, bf16[256,1024]{1,0:T(8,128)(2,1)S(1)}, u32[]{:S(2)}, u32[]{:S(2)}) collective-permute-start(bf16[256,1024]{1,0:T(8,128)(2,1)S(1)} %get-tuple-element.209.refs_0_), channel_id=1, source_target_pairs={{0,32},{4,36},{8,40},{12,44},{16,48},{20,52},{24,56},{28,60},{32,0... | collective-permute-start | bytes 1572872 | tf_op jit(solution)/shard_map/ppermute | solution.py:41
  183.7 13.3 %collective-permute-start.33 = (bf16[256,1024]{1,0:T(8,128)(2,1)S(1)}, bf16[256,1024]{1,0:T(8,128)(2,1)S(1)}, u32[]{:S(2)}, u32[]{:S(2)}) collective-permute-start(bf16[256,1024]{1,0:T(8,128)(2,1)S(1)} %get-tuple-element.209.refs_0_), channel_id=1, source_target_pairs={{0,16},{4,20},{8,24},{12,28},{16,32},{20,36},{24,40},{28,44},{32,4... | collective-permute-start | bytes 1572872 | tf_op jit(solution)/shard_map/ppermute | solution.py:41
  208.2 44.7 %collective-permute-start.44 = (bf16[768,1024]{1,0:T(8,128)(2,1)}, bf16[768,1024]{1,0:T(8,128)(2,1)S(1)}, u32[]{:S(2)}, u32[]{:S(2)}) collective-permute-start(bf16[768,1024]{1,0:T(8,128)(2,1)} %add_convert_fusion), channel_id=1, source_target_pairs={{0,2},{1,3},{2,0},{3,1},{4,6},{5,7},{6,4},{7,5},{8,10},{9,11},{10,... | collective-permute-start | bytes 4718600 | tf_op jit(solution)/shard_map/ppermute | solution.py:41
  208.6 15.3 %collective-permute-start.36 = (bf16[256,1024]{1,0:T(8,128)(2,1)S(1)}, bf16[256,1024]{1,0:T(8,128)(2,1)S(1)}, u32[]{:S(2)}, u32[]{:S(2)}) collective-permute-start(bf16[256,1024]{1,0:T(8,128)(2,1)S(1)} %get-tuple-element.219.refs_0_), channel_id=1, source_target_pairs={{0,4},{4,8},{8,12},{12,0},{16,20},{20,24},{24,28},{28,16},{32,36},... | collective-permute-start | bytes 1572872 | tf_op jit(solution)/shard_map/ppermute | solution.py:41
  210.6 13.8 %collective-permute-start.37 = (bf16[256,1024]{1,0:T(8,128)(2,1)S(1)}, bf16[256,1024]{1,0:T(8,128)(2,1)S(1)}, u32[]{:S(2)}, u32[]{:S(2)}) collective-permute-start(bf16[256,1024]{1,0:T(8,128)(2,1)S(1)} %get-tuple-element.219.refs_0_), channel_id=1, source_target_pairs={{0,12},{4,0},{8,4},{12,8},{16,28},{20,16},{24,20},{28,24},{32,44},... | collective-permute-start | bytes 1572872 | tf_op jit(solution)/shard_map/ppermute | solution.py:41
  211.8 15.5 %collective-permute-start.38 = (bf16[256,1024]{1,0:T(8,128)(2,1)S(1)}, bf16[256,1024]{1,0:T(8,128)(2,1)S(1)}, u32[]{:S(2)}, u32[]{:S(2)}) collective-permute-start(bf16[256,1024]{1,0:T(8,128)(2,1)S(1)} %get-tuple-element.221.refs_0_), channel_id=1, source_target_pairs={{0,16},{4,20},{8,24},{12,28},{16,32},{20,36},{24,40},{28,44},{32,4... | collective-permute-start | bytes 1572872 | tf_op jit(solution)/shard_map/ppermute | solution.py:41
  212.0 15.3 %collective-permute-start.39 = (bf16[256,1024]{1,0:T(8,128)(2,1)S(1)}, bf16[256,1024]{1,0:T(8,128)(2,1)S(1)}, u32[]{:S(2)}, u32[]{:S(2)}) collective-permute-start(bf16[256,1024]{1,0:T(8,128)(2,1)S(1)} %get-tuple-element.221.refs_0_), channel_id=1, source_target_pairs={{0,48},{4,52},{8,56},{12,60},{16,0},{20,4},{24,8},{28,12},{32,16},... | collective-permute-start | bytes 1572872 | tf_op jit(solution)/shard_map/ppermute | solution.py:41
  227.6 13.5 %collective-permute-start.40 = (bf16[128,1024]{1,0:T(8,128)(2,1)S(1)}, bf16[128,1024]{1,0:T(8,128)(2,1)S(1)}, u32[]{:S(2)}, u32[]{:S(2)}) collective-permute-start(bf16[128,1024]{1,0:T(8,128)(2,1)S(1)} %get-tuple-element.231), channel_id=1, source_target_pairs={{0,4},{4,8},{8,12},{12,0},{16,20},{20,24},{24,28},{28,16},{32,36},... | collective-permute-start | bytes 786440 | tf_op jit(solution)/shard_map/ppermute | solution.py:41
  227.7 13.4 %collective-permute-start.41 = (bf16[128,1024]{1,0:T(8,128)(2,1)S(1)}, bf16[128,1024]{1,0:T(8,128)(2,1)S(1)}, u32[]{:S(2)}, u32[]{:S(2)}) collective-permute-start(bf16[128,1024]{1,0:T(8,128)(2,1)S(1)} %get-tuple-element.232), channel_id=1, source_target_pairs={{0,12},{4,0},{8,4},{12,8},{16,28},{20,16},{24,20},{28,24},{32,44},... | collective-permute-start | bytes 786440 | tf_op jit(solution)/shard_map/ppermute | solution.py:41
  254.0 15.5 %collective-permute-start.48 = (bf16[768,1024]{1,0:T(8,128)(2,1)}, bf16[768,1024]{1,0:T(8,128)(2,1)}, u32[]{:S(2)}, u32[]{:S(2)}) collective-permute-start(bf16[768,1024]{1,0:T(8,128)(2,1)} %shard_map.73), channel_id=1, source_target_pairs={{0,1},{1,0},{2,3},{3,2},{4,5},{5,4},{6,7},{7,6},{8,9},{9,8},{10,11... | collective-permute-start | bytes 4718600 | tf_op jit(solution)/shard_map/ppermute | solution.py:41
  (45 other events, 330.4 us)

commit v3 on v2

--- a/solution.py
+++ b/solution.py
@@ -107,6 +107,7 @@
 
 small_cost = pl.CostEstimate(flops=1, bytes_accessed=1, transcendentals=0)
 params = pltpu.CompilerParams(vmem_limit_bytes=48 * 2**20)
+large = pltpu.CompilerParams(vmem_limit_bytes=56 * 2**20)
 over_columns = (((1,), (1,)), ((), ()))
 
 
@@ -249,7 +250,7 @@
         in_specs=[left, left, right, right] + ([tile, tile, line] if more else []),
         out_specs=tile,
         out_shape=jax.ShapeDtypeStruct((rows, width), low if more else full),
-        compiler_params=params,
+        compiler_params=large if more else params,
         cost_estimate=small_cost,
     )(low_even, low_odd, slope_even, slope_odd, *more)
 
@@ -290,7 +291,7 @@
         in_specs=[tile, whole(*slope.shape)] + [tile] * 3 + [whole(8, width)],
         out_specs=tile,
         out_shape=jax.ShapeDtypeStruct((rows, width), low),
-        compiler_params=params,
+        compiler_params=large,
         cost_estimate=small_cost,
     )(left, slope, near, across, view, stats)
 

time: 279 us -> 277 us (level)
  waiting for transfers between devices: 70.1 us -> 64 us
  other arithmetic: 11.9 us -> 17.9 us
    ppermute x49, waiting for transfers between devices: 57.8 us -> 51.7 us  [stage(): lax.ppermute(values, axis, [(d, place(d)) for d in range(count)])]
    unnamed x38 -> x34, local copies, waits for them, and re-layouts: 11 us -> 6.8 us
  transfers between devices with their start and end apart: 50 -> 50, of which waited for: 24 -> 24; matrix products, arithmetic and copies ran while one was open for 5% -> 7% of each run, Pallas kernels for 18% -> 19%
where the time goes in v3:
time: 277 us; the launch traced here: 275 us
  starting transfers between devices  83.6 us (30%)
  Pallas kernels  75.2 us (27%)
  waiting for transfers between devices  64 us (23%)
  other arithmetic  17.9 us (6%)
  blocking collectives  17.7 us (6%)
  local copies, waits for them, and re-layouts  10.1 us (4%)
  matrix products  5.72 us (2%)
    ppermute x49, starting transfers between devices, stage(): lax.ppermute(values, axis, [(d, place(d)) for d in range(count)])  80 us
    ppermute x49, waiting for transfers between devices, stage(): lax.ppermute(values, axis, [(d, place(d)) for d in range(count)])  51.7 us
    all_to_all x1, blocking collectives, share(): lax.all_to_all(pieces, 'dp', 0, 0, tiled=True, axis_index_groups=groups)  17.7 us
    pallas_call x2, Pallas kernels, up_a_call(): pl.pallas_call(grad_kernel if more else part_kernel, grid=(width // 256,)...  15.8 us
    pallas_call x4, Pallas kernels, slope_terms(): pl.pallas_call(terms_kernel, grid=(4,), in_specs=[tile, pl.BlockSpec((16,...  12.3 us
    all_to_all x1, waiting for transfers between devices, share(): lax.all_to_all(pieces, 'dp', 0, 0, tiled=True, axis_index_groups=groups)  12.3 us
    pallas_call x2, Pallas kernels, near_chunks(): pl.pallas_call(near_kernel, grid_spec=pltpu.PrefetchScalarGridSpec(num_sc...  10.1 us
    pallas_call x3, Pallas kernels, times(): pl.pallas_call(product_kernel, grid=(rows // 256,), in_specs=[pl.BlockSpe...  8.6 us
  transfers between devices with their start and end apart: 50, of which 24 were waited for; matrix products, arithmetic and copies ran while one was open for 7% of the time, Pallas kernels for 19%

profile of v3, /device:TPU:0, one launch (start us, length us, event | category | flops | bytes accessed | tf_op | source)
XLA Modules:
  0.0 275.4 jit_solution(7193549275048607893)
XLA Ops:
  6.9 17.7 %all_to_all.10 = f32[16,40,128]{2,1,0:T(8,128)S(1)} all-to-all(f32[16,40,128]{2,1,0:T(8,128)S(1)} %broadcast_in_dim.38), channel_id=1, replica_groups={{0,4,8,12,16,20,24,28,32,36,40,44,48,52,56,60},{64,68,72,76,80,84,88,92..., dimensions={0} | all-to-all | bytes 655360 | tf_op jit(solution)/shard_map/all_to_all | solution.py:52
  29.1 8.0 %collective-permute-done.view_c = bf16[768,1024]{1,0:T(8,128)(2,1)} collective-permute-done((bf16[768,1024]{1,0:T(8,128)(2,1)}, bf16[768,1024]{1,0:T(8,128)(2,1)}, u32[]{:S(2)}, u32[]{:S(2)}) %collective-permute-start) | collective-permute-done | bytes 1572896 | tf_op jit(solution)/shard_map/ppermute | solution.py:41
  38.2 3.3 %collective-permute-start.2 = (f32[5,1024]{1,0:T(8,128)S(1)}, f32[5,1024]{1,0:T(8,128)S(1)}, u32[]{:S(2)}, u32[]{:S(2)}) collective-permute-start(f32[5,1024]{1,0:T(8,128)S(1)} %pad_maximum_fusion.2), channel_id=1, source_target_pairs={{0,64},{4,68},{8,72},{12,76},{16,80},{20,84},{24,88},{28,92},{32,9... | collective-permute-start | bytes 61448 | tf_op jit(solution)/shard_map/ppermute | solution.py:41
  57.6 3.4 %shard_map.54 = (bf16[128,2048]{1,0:T(8,128)(2,1)}, bf16[128,2048]{1,0:T(8,128)(2,1)}) custom-call(s32[1]{0:T(128)} %bitcast.14.position, bf16[768,1024]{1,0:T(8,128)(2,1)S(1)} %get-tuple-element.261.left, bf16[768,2048]{1,0:T(8,128)(2,1)S(1)} %shard_map.50.right.odd), custom_call_target="tpu_custom_call" | custom-call | tf_op jit(solution)/shard_map/pallas_call | solution.py:193
  68.1 5.1 %shard_map.51 = (bf16[256,2048]{1,0:T(8,128)(2,1)}, bf16[256,2048]{1,0:T(8,128)(2,1)}) custom-call(s32[1]{0:T(128)} %bitcast.position, bf16[768,1024]{1,0:T(8,128)(2,1)S(1)} %get-tuple-element.261.left, bf16[768,2048]{1,0:T(8,128)(2,1)} %copy-done), custom_call_target="tpu_custom_call" | custom-call | tf_op jit(solution)/shard_map/pallas_call | solution.py:177
  73.2 5.1 %shard_map.52 = (bf16[256,2048]{1,0:T(8,128)(2,1)}, bf16[256,2048]{1,0:T(8,128)(2,1)}) custom-call(s32[1]{0:T(128)} %bitcast.10.position, bf16[768,1024]{1,0:T(8,128)(2,1)S(1)} %get-tuple-element.261.left, bf16[768,2048]{1,0:T(8,128)(2,1)} %copy-done.2), custom_call_target="tpu_custom_call" | custom-call | tf_op jit(solution)/shard_map/pallas_call | solution.py:177
  83.3 4.1 %shard_map.55 = (bf16[256,2048]{1,0:T(8,128)(2,1)}, bf16[256,2048]{1,0:T(8,128)(2,1)}, bf16[256,2048]{1,0:T(8,128)(2,1)}, bf16[256,2048]{1,0:T(8,128)(2,1)}) custom-call(bf16[256,2048]{1,0:T(8,128)(2,1)} %get-tuple-element.142.refs_0_, ...), custom_call_target="tpu_custom_call", output_to_operand_aliasing={{0}: (0, {}), {1}: (1, {}), {2}: (2, {}), {3}: (3, {})} | custom-call | tf_op jit(solution)/shard_map/pallas_call | solution.py:97
  87.5 3.2 %collective-permute-start.12 = (bf16[256,2048]{1,0:T(8,128)(2,1)}, bf16[256,2048]{1,0:T(8,128)(2,1)}, u32[]{:S(2)}, u32[]{:S(2)}) collective-permute-start(bf16[256,2048]{1,0:T(8,128)(2,1)} %get-tuple-element.159), channel_id=1, source_target_pairs={{0,12},{4,0},{8,4},{12,8},{16,28},{20,16},{24,20},{28,24},{32,44},... | collective-permute-start | bytes 3145736 | tf_op jit(solution)/shard_map/ppermute | solution.py:41
  90.7 3.2 %collective-permute-start.14 = (bf16[256,2048]{1,0:T(8,128)(2,1)}, bf16[256,2048]{1,0:T(8,128)(2,1)}, u32[]{:S(2)}, u32[]{:S(2)}) collective-permute-start(bf16[256,2048]{1,0:T(8,128)(2,1)} %get-tuple-element.161), channel_id=1, source_target_pairs={{0,48},{4,52},{8,56},{12,60},{16,0},{20,4},{24,8},{28,12},{32,16},... | collective-permute-start | bytes 3145736 | tf_op jit(solution)/shard_map/ppermute | solution.py:41
  99.5 3.5 %all-to-all-start.1 = ((f32[16,40,128]{2,1,0:T(8,128)}), f32[16,40,128]{2,1,0:T(8,128)S(1)}, u32[]{:S(2)}, u32[]{:S(2)}) async-start(f32[16,40,128]{2,1,0:T(8,128)} %broadcast_in_dim.40), calls=%async_computation.1 | async-start | bytes 655360 | tf_op jit(solution)/shard_map/all_to_all | solution.py:52
  103.1 3.3 %fusion.8.refs_3_ = f32[256,2048]{1,0:T(8,128)} fusion(bf16[768,2048]{1,0:T(8,128)(2,1)S(1)} %copy-done.4, bf16[768,1024]{1,0:T(8,128)(2,1)} %copy-done.5, s32[]{:T(128)S(6)} %select_n.7), kind=kOutput, calls=%fused_computation.20 | convolution fusion | flops 805306368 | bytes 5636100 | tf_op jit(solution)/shard_map/dot_general | solution.py:493
  106.4 12.3 %all-to-all-done.1 = f32[16,40,128]{2,1,0:T(8,128)S(1)} async-done(((f32[16,40,128]{2,1,0:T(8,128)}), f32[16,40,128]{2,1,0:T(8,128)S(1)}, u32[]{:S(2)}, u32[]{:S(2)}) %all-to-all-start.1) | async-done | bytes 327712 | tf_op jit(solution)/shard_map/all_to_all | solution.py:52
  118.7 5.0 %shard_map.56 = (f32[64,2048]{1,0:T(8,128)S(1)}, bf16[64,2048]{1,0:T(8,128)(2,1)S(1)}, bf16[64,2048]{1,0:T(8,128)(2,1)S(1)}, bf16[64,2048]{1,0:T(8,128)(2,1)S(1)...) custom-call(s32[2]{0:T(128)S(1)} %pad_add_fusion.places, ...), custom_call_target="tpu_custom_call" | custom-call | tf_op jit(solution)/shard_map/pallas_call | solution.py:320
  133.1 3.4 %collective-permute-start.20 = (bf16[64,2048]{1,0:T(8,128)(2,1)S(1)}, bf16[64,2048]{1,0:T(8,128)(2,1)S(1)}, u32[]{:S(2)}, u32[]{:S(2)}) collective-permute-start(bf16[64,2048]{1,0:T(8,128)(2,1)S(1)} %get-tuple-element.180), channel_id=1, source_target_pairs={{0,12},{4,0},{8,4},{12,8},{16,28},{20,16},{24,20},{28,24},{32,44},... | collective-permute-start | bytes 786440 | tf_op jit(solution)/shard_map/ppermute | solution.py:41
  146.3 8.6 %collective-permute-done.22 = f32[40,128]{1,0:T(8,128)S(1)} collective-permute-done((f32[40,128]{1,0:T(8,128)S(1)}, f32[40,128]{1,0:T(8,128)S(1)}, u32[]{:S(2)}, u32[]{:S(2)}) %collective-permute-start.22) | collective-permute-done | bytes 20512 | tf_op jit(solution)/shard_map/ppermute | solution.py:41
  176.1 7.5 %collective-permute-start.32 = (bf16[256,1024]{1,0:T(8,128)(2,1)S(1)}, bf16[256,1024]{1,0:T(8,128)(2,1)S(1)}, u32[]{:S(2)}, u32[]{:S(2)}) collective-permute-start(bf16[256,1024]{1,0:T(8,128)(2,1)S(1)} %get-tuple-element.209.refs_0_), channel_id=1, source_target_pairs={{0,32},{4,36},{8,40},{12,44},{16,48},{20,52},{24,56},{28,60},{32,0... | collective-permute-start | bytes 1572872 | tf_op jit(solution)/shard_map/ppermute | solution.py:41
  187.5 3.7 %collective-permute-start.34 = (bf16[256,1024]{1,0:T(8,128)(2,1)S(1)}, bf16[256,1024]{1,0:T(8,128)(2,1)S(1)}, u32[]{:S(2)}, u32[]{:S(2)}) collective-permute-start(bf16[256,1024]{1,0:T(8,128)(2,1)S(1)} %get-tuple-element.209.refs_0_), channel_id=1, source_target_pairs={{0,48},{4,52},{8,56},{12,60},{16,0},{20,4},{24,8},{28,12},{32,16},... | collective-permute-start | bytes 1572872 | tf_op jit(solution)/shard_map/ppermute | solution.py:41
  201.4 3.4 %shard_map.61 = f32[768,1024]{1,0:T(8,128)} custom-call(bf16[768,1024]{1,0:T(8,128)(2,1)S(1)} %copy-done.6, bf16[1024,1024]{1,0:T(8,128)(2,1)S(1)} %shard_map.60.right.slope.slope_even), custom_call_target="tpu_custom_call" | custom-call | flops 1 | bytes 1 | tf_op jit(solution)/shard_map/pallas_call | solution.py:213
  204.8 3.6 %add_convert_fusion = bf16[768,1024]{1,0:T(8,128)(2,1)} fusion(f32[768,1024]{1,0:T(8,128)} %shard_map.61, bf16[768,1024]{1,0:T(8,128)(2,1)S(1)} %collective-permute-done.35), kind=kLoop, calls=%fused_computation.15 | loop fusion | flops 2359296 | bytes 6291456 | tf_op jit(solution)/shard_map/convert_element_type | solution.py:558
  211.9 3.3 %collective-permute-start.39 = (bf16[256,1024]{1,0:T(8,128)(2,1)S(1)}, bf16[256,1024]{1,0:T(8,128)(2,1)S(1)}, u32[]{:S(2)}, u32[]{:S(2)}) collective-permute-start(bf16[256,1024]{1,0:T(8,128)(2,1)S(1)} %get-tuple-element.221.refs_0_), channel_id=1, source_target_pairs={{0,48},{4,52},{8,56},{12,60},{16,0},{20,4},{24,8},{28,12},{32,16},... | collective-permute-start | bytes 1572872 | tf_op jit(solution)/shard_map/ppermute | solution.py:41
  234.2 7.0 %shard_map.67.part = f32[768,1024]{1,0:T(8,128)} custom-call(bf16[768,2048]{1,0:T(8,128)(2,1)} %copy-done, bf16[768,2048]{1,0:T(8,128)(2,1)} %copy-done.2, bf16[1024,1024]{1,0:T(8,128)(2,1)S(1)} %shard_map.60.right.slope.slope_even, bf16[1024,1024]{1,0:T(8,128)(2,1)S(1)} %shard_map.62.right.slope.slope_odd), custom_call_target="tpu_custom_call" | custom-call | flops 1 | bytes 1 | tf_op jit(solution)/shard_map/pallas_call | solution.py:247
  247.6 4.0 %shard_map.69 = (f32[8,1024]{1,0:T(8,128)S(1)}, f32[8,1024]{1,0:T(8,128)S(1)}, bf16[1024,1024]{1,0:T(8,128)(2,1)S(1)}) custom-call(bf16[1024,1024]{1,0:T(8,128)(2,1)S(1)} %shard_map.68.slope, bf16[16,1024]{1,0:T(8,128)(2,1)S(1)} %broadcast_in_dim.41.weights, bf16[16,1024]{1,0:T(8,128)(2,1)S(1)} %broadcast_in_dim.44.means, ...), custom_call_target="tpu_custom_call", output_to_operand_aliasing={{2}: (0, {})} | custom-call | flops 1 | bytes 1 | tf_op jit(solution)/shard_map/pallas_call | solution.py:372
  256.7 8.8 %shard_map.72 = bf16[768,1024]{1,0:T(8,128)(2,1)} custom-call(bf16[768,2048]{1,0:T(8,128)(2,1)} %copy-done, bf16[768,2048]{1,0:T(8,128)(2,1)} %copy-done.2, bf16[1024,1024]{1,0:T(8,128)(2,1)} %copy-done.7, bf16[1024,1024]{1,0:T(8,128)(2,1)} %copy-done.8, f32[768,1024]{1,0:T(8,128)} %shard_map.67.part, bf16[768,1024]{1,0:T(8,128)(2,1)} %view.2, ...), custom_call_target="tpu_custom_call" | custom-call | flops 1 | bytes 1 | tf_op jit(solution)/shard_map/pallas_call | solution.py:247
  268.6 6.7 %shard_map.74 = bf16[768,1024]{1,0:T(8,128)(2,1)} custom-call(bf16[768,1024]{1,0:T(8,128)(2,1)} %copy-done.5, bf16[1024,1024]{1,0:T(8,128)(2,1)} %copy-done.7, bf16[768,1024]{1,0:T(8,128)(2,1)} %copy-done.16, bf16[768,1024]{1,0:T(8,128)(2,1)} %copy-done.15, bf16[768,1024]{1,0:T(8,128)(2,1)} %view.3, f32[8,1024]{1,0:T(8,128)} %concatenate.31.stats), custom_call_target="tpu_custom_call" | custom-call | flops 1 | bytes 1 | tf_op jit(solution)/shard_map/pallas_call | solution.py:288
  (205 shorter events, 137.0 us)
Async XLA Ops:
  0.7 36.4 %collective-permute-start = (bf16[768,1024]{1,0:T(8,128)(2,1)}, bf16[768,1024]{1,0:T(8,128)(2,1)}, u32[]{:S(2)}, u32[]{:S(2)}) collective-permute-start(bf16[768,1024]{1,0:T(8,128)(2,1)} %view.3), channel_id=1, source_target_pairs={{0,2},{1,3},{2,0},{3,1},{4,6},{5,7},{6,4},{7,5},{8,10},{9,11},{10,... | collective-permute-start | bytes 4718600 | tf_op jit(solution)/shard_map/ppermute | solution.py:41
  2.3 34.7 %collective-permute-start.1 = (bf16[768,1024]{1,0:T(8,128)(2,1)}, bf16[768,1024]{1,0:T(8,128)(2,1)S(1)}, u32[]{:S(2)}, u32[]{:S(2)}) collective-permute-start(bf16[768,1024]{1,0:T(8,128)(2,1)} %view.3), channel_id=1, source_target_pairs={{0,1},{1,0},{2,3},{3,2},{4,5},{5,4},{6,7},{7,6},{8,9},{9,8},{10,11... | collective-permute-start | bytes 4718600 | tf_op jit(solution)/shard_map/ppermute | solution.py:41
  60.9 17.3 %collective-permute-start.10 = (bf16[128,2048]{1,0:T(8,128)(2,1)}, bf16[128,2048]{1,0:T(8,128)(2,1)S(1)}, u32[]{:S(2)}, u32[]{:S(2)}) collective-permute-start(bf16[128,2048]{1,0:T(8,128)(2,1)} %get-tuple-element.153), channel_id=1, source_target_pairs={{0,48},{4,52},{8,56},{12,60},{16,0},{20,4},{24,8},{28,12},{32,16},... | collective-permute-start | bytes 1572872 | tf_op jit(solution)/shard_map/ppermute | solution.py:41
  64.0 16.6 %collective-permute-start.7 = (bf16[128,2048]{1,0:T(8,128)(2,1)}, bf16[128,2048]{1,0:T(8,128)(2,1)S(1)}, u32[]{:S(2)}, u32[]{:S(2)}) collective-permute-start(bf16[128,2048]{1,0:T(8,128)(2,1)} %get-tuple-element.150), channel_id=1, source_target_pairs={{0,4},{4,8},{8,12},{12,0},{16,20},{20,24},{24,28},{28,16},{32,36},... | collective-permute-start | bytes 1572872 | tf_op jit(solution)/shard_map/ppermute | solution.py:41
  65.9 14.6 %collective-permute-start.8 = (bf16[128,2048]{1,0:T(8,128)(2,1)}, bf16[128,2048]{1,0:T(8,128)(2,1)S(1)}, u32[]{:S(2)}, u32[]{:S(2)}) collective-permute-start(bf16[128,2048]{1,0:T(8,128)(2,1)} %get-tuple-element.151), channel_id=1, source_target_pairs={{0,12},{4,0},{8,4},{12,8},{16,28},{20,16},{24,20},{28,24},{32,44},... | collective-permute-start | bytes 1572872 | tf_op jit(solution)/shard_map/ppermute | solution.py:41
  68.1 15.3 %collective-permute-start.9 = (bf16[128,2048]{1,0:T(8,128)(2,1)}, bf16[128,2048]{1,0:T(8,128)(2,1)}, u32[]{:S(2)}, u32[]{:S(2)}) collective-permute-start(bf16[128,2048]{1,0:T(8,128)(2,1)} %get-tuple-element.152), channel_id=1, source_target_pairs={{0,16},{4,20},{8,24},{12,28},{16,32},{20,36},{24,40},{28,44},{32,4... | collective-permute-start | bytes 1572872 | tf_op jit(solution)/shard_map/ppermute | solution.py:41
  87.5 31.2 %collective-permute-start.11 = (bf16[256,2048]{1,0:T(8,128)(2,1)}, bf16[256,2048]{1,0:T(8,128)(2,1)}, u32[]{:S(2)}, u32[]{:S(2)}) collective-permute-start(bf16[256,2048]{1,0:T(8,128)(2,1)} %get-tuple-element.158), channel_id=1, source_target_pairs={{0,4},{4,8},{8,12},{12,0},{16,20},{20,24},{24,28},{28,16},{32,36},... | collective-permute-start | bytes 3145736 | tf_op jit(solution)/shard_map/ppermute | solution.py:41
  87.5 31.2 %collective-permute-start.12 = (bf16[256,2048]{1,0:T(8,128)(2,1)}, bf16[256,2048]{1,0:T(8,128)(2,1)}, u32[]{:S(2)}, u32[]{:S(2)}) collective-permute-start(bf16[256,2048]{1,0:T(8,128)(2,1)} %get-tuple-element.159), channel_id=1, source_target_pairs={{0,12},{4,0},{8,4},{12,8},{16,28},{20,16},{24,20},{28,24},{32,44},... | collective-permute-start | bytes 3145736 | tf_op jit(solution)/shard_map/ppermute | solution.py:41
  90.7 28.0 %collective-permute-start.13 = (bf16[256,2048]{1,0:T(8,128)(2,1)}, bf16[256,2048]{1,0:T(8,128)(2,1)}, u32[]{:S(2)}, u32[]{:S(2)}) collective-permute-start(bf16[256,2048]{1,0:T(8,128)(2,1)} %get-tuple-element.160), channel_id=1, source_target_pairs={{0,16},{4,20},{8,24},{12,28},{16,32},{20,36},{24,40},{28,44},{32,4... | collective-permute-start | bytes 3145736 | tf_op jit(solution)/shard_map/ppermute | solution.py:41
  90.7 28.0 %collective-permute-start.14 = (bf16[256,2048]{1,0:T(8,128)(2,1)}, bf16[256,2048]{1,0:T(8,128)(2,1)}, u32[]{:S(2)}, u32[]{:S(2)}) collective-permute-start(bf16[256,2048]{1,0:T(8,128)(2,1)} %get-tuple-element.161), channel_id=1, source_target_pairs={{0,48},{4,52},{8,56},{12,60},{16,0},{20,4},{24,8},{28,12},{32,16},... | collective-permute-start | bytes 3145736 | tf_op jit(solution)/shard_map/ppermute | solution.py:41
  99.5 19.2 %all-to-all-start.1 = ((f32[16,40,128]{2,1,0:T(8,128)}), f32[16,40,128]{2,1,0:T(8,128)S(1)}, u32[]{:S(2)}, u32[]{:S(2)}) async-start(f32[16,40,128]{2,1,0:T(8,128)} %broadcast_in_dim.40), calls=%async_computation.1 | async-start | bytes 655360 | tf_op jit(solution)/shard_map/all_to_all | solution.py:52
  171.7 15.8 %collective-permute-start.29 = (bf16[256,1024]{1,0:T(8,128)(2,1)S(1)}, bf16[256,1024]{1,0:T(8,128)(2,1)S(1)}, u32[]{:S(2)}, u32[]{:S(2)}) collective-permute-start(bf16[256,1024]{1,0:T(8,128)(2,1)S(1)} %get-tuple-element.206.refs_0_), channel_id=1, source_target_pairs={{0,8},{4,12},{8,0},{12,4},{16,24},{20,28},{24,16},{28,20},{32,40},... | collective-permute-start | bytes 1572872 | tf_op jit(solution)/shard_map/ppermute | solution.py:41
  172.9 20.1 %collective-permute-start.30 = (bf16[256,1024]{1,0:T(8,128)(2,1)S(1)}, bf16[256,1024]{1,0:T(8,128)(2,1)S(1)}, u32[]{:S(2)}, u32[]{:S(2)}) collective-permute-start(bf16[256,1024]{1,0:T(8,128)(2,1)S(1)} %get-tuple-element.206.refs_0_), channel_id=1, source_target_pairs={{0,4},{4,8},{8,12},{12,0},{16,20},{20,24},{24,28},{28,16},{32,36},... | collective-permute-start | bytes 1572872 | tf_op jit(solution)/shard_map/ppermute | solution.py:41
  175.5 18.4 %collective-permute-start.31 = (bf16[256,1024]{1,0:T(8,128)(2,1)S(1)}, bf16[256,1024]{1,0:T(8,128)(2,1)S(1)}, u32[]{:S(2)}, u32[]{:S(2)}) collective-permute-start(bf16[256,1024]{1,0:T(8,128)(2,1)S(1)} %get-tuple-element.206.refs_0_), channel_id=1, source_target_pairs={{0,12},{4,0},{8,4},{12,8},{16,28},{20,16},{24,20},{28,24},{32,44},... | collective-permute-start | bytes 1572872 | tf_op jit(solution)/shard_map/ppermute | solution.py:41
  176.1 17.8 %collective-permute-start.32 = (bf16[256,1024]{1,0:T(8,128)(2,1)S(1)}, bf16[256,1024]{1,0:T(8,128)(2,1)S(1)}, u32[]{:S(2)}, u32[]{:S(2)}) collective-permute-start(bf16[256,1024]{1,0:T(8,128)(2,1)S(1)} %get-tuple-element.209.refs_0_), channel_id=1, source_target_pairs={{0,32},{4,36},{8,40},{12,44},{16,48},{20,52},{24,56},{28,60},{32,0... | collective-permute-start | bytes 1572872 | tf_op jit(solution)/shard_map/ppermute | solution.py:41
  183.6 13.3 %collective-permute-start.33 = (bf16[256,1024]{1,0:T(8,128)(2,1)S(1)}, bf16[256,1024]{1,0:T(8,128)(2,1)S(1)}, u32[]{:S(2)}, u32[]{:S(2)}) collective-permute-start(bf16[256,1024]{1,0:T(8,128)(2,1)S(1)} %get-tuple-element.209.refs_0_), channel_id=1, source_target_pairs={{0,16},{4,20},{8,24},{12,28},{16,32},{20,36},{24,40},{28,44},{32,4... | collective-permute-start | bytes 1572872 | tf_op jit(solution)/shard_map/ppermute | solution.py:41
  208.4 44.5 %collective-permute-start.44 = (bf16[768,1024]{1,0:T(8,128)(2,1)}, bf16[768,1024]{1,0:T(8,128)(2,1)S(1)}, u32[]{:S(2)}, u32[]{:S(2)}) collective-permute-start(bf16[768,1024]{1,0:T(8,128)(2,1)} %add_convert_fusion), channel_id=1, source_target_pairs={{0,2},{1,3},{2,0},{3,1},{4,6},{5,7},{6,4},{7,5},{8,10},{9,11},{10,... | collective-permute-start | bytes 4718600 | tf_op jit(solution)/shard_map/ppermute | solution.py:41
  208.6 15.4 %collective-permute-start.36 = (bf16[256,1024]{1,0:T(8,128)(2,1)S(1)}, bf16[256,1024]{1,0:T(8,128)(2,1)S(1)}, u32[]{:S(2)}, u32[]{:S(2)}) collective-permute-start(bf16[256,1024]{1,0:T(8,128)(2,1)S(1)} %get-tuple-element.219.refs_0_), channel_id=1, source_target_pairs={{0,4},{4,8},{8,12},{12,0},{16,20},{20,24},{24,28},{28,16},{32,36},... | collective-permute-start | bytes 1572872 | tf_op jit(solution)/shard_map/ppermute | solution.py:41
  210.6 13.8 %collective-permute-start.37 = (bf16[256,1024]{1,0:T(8,128)(2,1)S(1)}, bf16[256,1024]{1,0:T(8,128)(2,1)S(1)}, u32[]{:S(2)}, u32[]{:S(2)}) collective-permute-start(bf16[256,1024]{1,0:T(8,128)(2,1)S(1)} %get-tuple-element.219.refs_0_), channel_id=1, source_target_pairs={{0,12},{4,0},{8,4},{12,8},{16,28},{20,16},{24,20},{28,24},{32,44},... | collective-permute-start | bytes 1572872 | tf_op jit(solution)/shard_map/ppermute | solution.py:41
  211.8 15.5 %collective-permute-start.38 = (bf16[256,1024]{1,0:T(8,128)(2,1)S(1)}, bf16[256,1024]{1,0:T(8,128)(2,1)S(1)}, u32[]{:S(2)}, u32[]{:S(2)}) collective-permute-start(bf16[256,1024]{1,0:T(8,128)(2,1)S(1)} %get-tuple-element.221.refs_0_), channel_id=1, source_target_pairs={{0,16},{4,20},{8,24},{12,28},{16,32},{20,36},{24,40},{28,44},{32,4... | collective-permute-start | bytes 1572872 | tf_op jit(solution)/shard_map/ppermute | solution.py:41
  211.9 15.4 %collective-permute-start.39 = (bf16[256,1024]{1,0:T(8,128)(2,1)S(1)}, bf16[256,1024]{1,0:T(8,128)(2,1)S(1)}, u32[]{:S(2)}, u32[]{:S(2)}) collective-permute-start(bf16[256,1024]{1,0:T(8,128)(2,1)S(1)} %get-tuple-element.221.refs_0_), channel_id=1, source_target_pairs={{0,48},{4,52},{8,56},{12,60},{16,0},{20,4},{24,8},{28,12},{32,16},... | collective-permute-start | bytes 1572872 | tf_op jit(solution)/shard_map/ppermute | solution.py:41
  227.6 13.5 %collective-permute-start.40 = (bf16[128,1024]{1,0:T(8,128)(2,1)S(1)}, bf16[128,1024]{1,0:T(8,128)(2,1)S(1)}, u32[]{:S(2)}, u32[]{:S(2)}) collective-permute-start(bf16[128,1024]{1,0:T(8,128)(2,1)S(1)} %get-tuple-element.231), channel_id=1, source_target_pairs={{0,4},{4,8},{8,12},{12,0},{16,20},{20,24},{24,28},{28,16},{32,36},... | collective-permute-start | bytes 786440 | tf_op jit(solution)/shard_map/ppermute | solution.py:41
  227.7 13.4 %collective-permute-start.41 = (bf16[128,1024]{1,0:T(8,128)(2,1)S(1)}, bf16[128,1024]{1,0:T(8,128)(2,1)S(1)}, u32[]{:S(2)}, u32[]{:S(2)}) collective-permute-start(bf16[128,1024]{1,0:T(8,128)(2,1)S(1)} %get-tuple-element.232), channel_id=1, source_target_pairs={{0,12},{4,0},{8,4},{12,8},{16,28},{20,16},{24,20},{28,24},{32,44},... | collective-permute-start | bytes 786440 | tf_op jit(solution)/shard_map/ppermute | solution.py:41
  253.0 14.4 %collective-permute-start.48 = (bf16[768,1024]{1,0:T(8,128)(2,1)}, bf16[768,1024]{1,0:T(8,128)(2,1)S(1)}, u32[]{:S(2)}, u32[]{:S(2)}) collective-permute-start(bf16[768,1024]{1,0:T(8,128)(2,1)} %shard_map.73), channel_id=1, source_target_pairs={{0,1},{1,0},{2,3},{3,2},{4,5},{5,4},{6,7},{7,6},{8,9},{9,8},{10,11... | collective-permute-start | bytes 4718600 | tf_op jit(solution)/shard_map/ppermute | solution.py:41
  (43 other events, 322.3 us)

commit v4 on v3

--- a/solution.py
+++ b/solution.py
@@ -93,11 +93,11 @@
 
 def add_halves(blocks, received):
     rows, columns = received[0].shape
-    halves = [pl.BlockSpec((rows, 512), lambda i, h=h: (h, i)) for h in (0, 1, 0, 1)]
+    halves = [pl.BlockSpec((rows, 1024), lambda i, h=h: (h, i)) for h in (0, 1, 0, 1)]
     return pl.pallas_call(
         add_kernel,
-        grid=(columns // 512,),
-        in_specs=halves + [pl.BlockSpec((rows, 512), lambda i: (0, i))] * 4,
+        grid=(columns // 1024,),
+        in_specs=halves + [pl.BlockSpec((rows, 1024), lambda i: (0, i))] * 4,
         out_specs=halves,
         out_shape=[jax.ShapeDtypeStruct(block.shape, low) for block in blocks],
         input_output_aliases={index: index for index in range(4)},

time: 277 us -> 276 us (level)
  transfers between devices with their start and end apart: 50 -> 50, of which waited for: 24 -> 24; matrix products, arithmetic and copies ran while one was open for 7% -> 8% of each run, Pallas kernels for 19% -> 19%
where the time goes in v4:
time: 276 us; the launch traced here: 274 us
  starting transfers between devices  83.6 us (30%)
  Pallas kernels  74 us (27%)
  waiting for transfers between devices  64 us (23%)
  other arithmetic  17.9 us (6%)
  blocking collectives  17.7 us (6%)
  local copies, waits for them, and re-layouts  10.1 us (4%)
  matrix products  5.72 us (2%)
    ppermute x49, starting transfers between devices, stage(): lax.ppermute(values, axis, [(d, place(d)) for d in range(count)])  80.1 us
    ppermute x49, waiting for transfers between devices, stage(): lax.ppermute(values, axis, [(d, place(d)) for d in range(count)])  51.7 us
    all_to_all x1, blocking collectives, share(): lax.all_to_all(pieces, 'dp', 0, 0, tiled=True, axis_index_groups=groups)  17.7 us
    pallas_call x2, Pallas kernels, up_a_call(): pl.pallas_call(grad_kernel if more else part_kernel, grid=(width // 256,)...  15.8 us
    pallas_call x4, Pallas kernels, slope_terms(): pl.pallas_call(terms_kernel, grid=(4,), in_specs=[tile, pl.BlockSpec((16,...  12.3 us
    all_to_all x1, waiting for transfers between devices, share(): lax.all_to_all(pieces, 'dp', 0, 0, tiled=True, axis_index_groups=groups)  12.3 us
    pallas_call x2, Pallas kernels, near_chunks(): pl.pallas_call(near_kernel, grid_spec=pltpu.PrefetchScalarGridSpec(num_sc...  10.1 us
    pallas_call x3, Pallas kernels, times(): pl.pallas_call(product_kernel, grid=(rows // 256,), in_specs=[pl.BlockSpe...  8.59 us
  transfers between devices with their start and end apart: 50, of which 24 were waited for; matrix products, arithmetic and copies ran while one was open for 8% of the time, Pallas kernels for 19%

profile of v4, /device:TPU:0, one launch (start us, length us, event | category | flops | bytes accessed | tf_op | source)
XLA Modules:
  0.0 274.2 jit_solution(4219287142524478109)
XLA Ops:
  6.9 17.7 %all_to_all.10 = f32[16,40,128]{2,1,0:T(8,128)S(1)} all-to-all(f32[16,40,128]{2,1,0:T(8,128)S(1)} %broadcast_in_dim.38), channel_id=1, replica_groups={{0,4,8,12,16,20,24,28,32,36,40,44,48,52,56,60},{64,68,72,76,80,84,88,92..., dimensions={0} | all-to-all | bytes 655360 | tf_op jit(solution)/shard_map/all_to_all | solution.py:52
  29.1 8.0 %collective-permute-done.view_c = bf16[768,1024]{1,0:T(8,128)(2,1)} collective-permute-done((bf16[768,1024]{1,0:T(8,128)(2,1)}, bf16[768,1024]{1,0:T(8,128)(2,1)}, u32[]{:S(2)}, u32[]{:S(2)}) %collective-permute-start) | collective-permute-done | bytes 1572896 | tf_op jit(solution)/shard_map/ppermute | solution.py:41
  38.2 3.3 %collective-permute-start.2 = (f32[5,1024]{1,0:T(8,128)S(1)}, f32[5,1024]{1,0:T(8,128)S(1)}, u32[]{:S(2)}, u32[]{:S(2)}) collective-permute-start(f32[5,1024]{1,0:T(8,128)S(1)} %pad_maximum_fusion.2), channel_id=1, source_target_pairs={{0,64},{4,68},{8,72},{12,76},{16,80},{20,84},{24,88},{28,92},{32,9... | collective-permute-start | bytes 61448 | tf_op jit(solution)/shard_map/ppermute | solution.py:41
  57.6 3.4 %shard_map.54 = (bf16[128,2048]{1,0:T(8,128)(2,1)}, bf16[128,2048]{1,0:T(8,128)(2,1)}) custom-call(s32[1]{0:T(128)} %bitcast.14.position, bf16[768,1024]{1,0:T(8,128)(2,1)S(1)} %get-tuple-element.261.left, bf16[768,2048]{1,0:T(8,128)(2,1)S(1)} %shard_map.50.right.odd), custom_call_target="tpu_custom_call" | custom-call | tf_op jit(solution)/shard_map/pallas_call | solution.py:193
  68.1 5.1 %shard_map.51 = (bf16[256,2048]{1,0:T(8,128)(2,1)}, bf16[256,2048]{1,0:T(8,128)(2,1)}) custom-call(s32[1]{0:T(128)} %bitcast.position, bf16[768,1024]{1,0:T(8,128)(2,1)S(1)} %get-tuple-element.261.left, bf16[768,2048]{1,0:T(8,128)(2,1)} %copy-done), custom_call_target="tpu_custom_call" | custom-call | tf_op jit(solution)/shard_map/pallas_call | solution.py:177
  73.2 5.1 %shard_map.52 = (bf16[256,2048]{1,0:T(8,128)(2,1)}, bf16[256,2048]{1,0:T(8,128)(2,1)}) custom-call(s32[1]{0:T(128)} %bitcast.10.position, bf16[768,1024]{1,0:T(8,128)(2,1)S(1)} %get-tuple-element.261.left, bf16[768,2048]{1,0:T(8,128)(2,1)} %copy-done.2), custom_call_target="tpu_custom_call" | custom-call | tf_op jit(solution)/shard_map/pallas_call | solution.py:177
  86.3 3.2 %collective-permute-start.12 = (bf16[256,2048]{1,0:T(8,128)(2,1)}, bf16[256,2048]{1,0:T(8,128)(2,1)}, u32[]{:S(2)}, u32[]{:S(2)}) collective-permute-start(bf16[256,2048]{1,0:T(8,128)(2,1)} %get-tuple-element.159), channel_id=1, source_target_pairs={{0,12},{4,0},{8,4},{12,8},{16,28},{20,16},{24,20},{28,24},{32,44},... | collective-permute-start | bytes 3145736 | tf_op jit(solution)/shard_map/ppermute | solution.py:41
  89.6 3.2 %collective-permute-start.14 = (bf16[256,2048]{1,0:T(8,128)(2,1)}, bf16[256,2048]{1,0:T(8,128)(2,1)}, u32[]{:S(2)}, u32[]{:S(2)}) collective-permute-start(bf16[256,2048]{1,0:T(8,128)(2,1)} %get-tuple-element.161), channel_id=1, source_target_pairs={{0,48},{4,52},{8,56},{12,60},{16,0},{20,4},{24,8},{28,12},{32,16},... | collective-permute-start | bytes 3145736 | tf_op jit(solution)/shard_map/ppermute | solution.py:41
  98.4 3.5 %all-to-all-start.1 = ((f32[16,40,128]{2,1,0:T(8,128)}), f32[16,40,128]{2,1,0:T(8,128)S(1)}, u32[]{:S(2)}, u32[]{:S(2)}) async-start(f32[16,40,128]{2,1,0:T(8,128)} %broadcast_in_dim.40), calls=%async_computation.1 | async-start | bytes 655360 | tf_op jit(solution)/shard_map/all_to_all | solution.py:52
  101.9 3.3 %fusion.8.refs_3_ = f32[256,2048]{1,0:T(8,128)} fusion(bf16[768,2048]{1,0:T(8,128)(2,1)S(1)} %copy-done.4, bf16[768,1024]{1,0:T(8,128)(2,1)} %copy-done.5, s32[]{:T(128)S(6)} %select_n.7), kind=kOutput, calls=%fused_computation.20 | convolution fusion | flops 805306368 | bytes 5636100 | tf_op jit(solution)/shard_map/dot_general | solution.py:493
  105.2 12.3 %all-to-all-done.1 = f32[16,40,128]{2,1,0:T(8,128)S(1)} async-done(((f32[16,40,128]{2,1,0:T(8,128)}), f32[16,40,128]{2,1,0:T(8,128)S(1)}, u32[]{:S(2)}, u32[]{:S(2)}) %all-to-all-start.1) | async-done | bytes 327712 | tf_op jit(solution)/shard_map/all_to_all | solution.py:52
  117.6 5.0 %shard_map.56 = (f32[64,2048]{1,0:T(8,128)S(1)}, bf16[64,2048]{1,0:T(8,128)(2,1)S(1)}, bf16[64,2048]{1,0:T(8,128)(2,1)S(1)}, bf16[64,2048]{1,0:T(8,128)(2,1)S(1)...) custom-call(s32[2]{0:T(128)S(1)} %pad_add_fusion.places, ...), custom_call_target="tpu_custom_call" | custom-call | tf_op jit(solution)/shard_map/pallas_call | solution.py:320
  131.9 3.4 %collective-permute-start.20 = (bf16[64,2048]{1,0:T(8,128)(2,1)S(1)}, bf16[64,2048]{1,0:T(8,128)(2,1)S(1)}, u32[]{:S(2)}, u32[]{:S(2)}) collective-permute-start(bf16[64,2048]{1,0:T(8,128)(2,1)S(1)} %get-tuple-element.180), channel_id=1, source_target_pairs={{0,12},{4,0},{8,4},{12,8},{16,28},{20,16},{24,20},{28,24},{32,44},... | collective-permute-start | bytes 786440 | tf_op jit(solution)/shard_map/ppermute | solution.py:41
  145.1 8.6 %collective-permute-done.22 = f32[40,128]{1,0:T(8,128)S(1)} collective-permute-done((f32[40,128]{1,0:T(8,128)S(1)}, f32[40,128]{1,0:T(8,128)S(1)}, u32[]{:S(2)}, u32[]{:S(2)}) %collective-permute-start.22) | collective-permute-done | bytes 20512 | tf_op jit(solution)/shard_map/ppermute | solution.py:41
  174.9 7.5 %collective-permute-start.32 = (bf16[256,1024]{1,0:T(8,128)(2,1)S(1)}, bf16[256,1024]{1,0:T(8,128)(2,1)S(1)}, u32[]{:S(2)}, u32[]{:S(2)}) collective-permute-start(bf16[256,1024]{1,0:T(8,128)(2,1)S(1)} %get-tuple-element.209.refs_0_), channel_id=1, source_target_pairs={{0,32},{4,36},{8,40},{12,44},{16,48},{20,52},{24,56},{28,60},{32,0... | collective-permute-start | bytes 1572872 | tf_op jit(solution)/shard_map/ppermute | solution.py:41
  186.3 3.7 %collective-permute-start.34 = (bf16[256,1024]{1,0:T(8,128)(2,1)S(1)}, bf16[256,1024]{1,0:T(8,128)(2,1)S(1)}, u32[]{:S(2)}, u32[]{:S(2)}) collective-permute-start(bf16[256,1024]{1,0:T(8,128)(2,1)S(1)} %get-tuple-element.209.refs_0_), channel_id=1, source_target_pairs={{0,48},{4,52},{8,56},{12,60},{16,0},{20,4},{24,8},{28,12},{32,16},... | collective-permute-start | bytes 1572872 | tf_op jit(solution)/shard_map/ppermute | solution.py:41
  200.2 3.4 %shard_map.61 = f32[768,1024]{1,0:T(8,128)} custom-call(bf16[768,1024]{1,0:T(8,128)(2,1)S(1)} %copy-done.6, bf16[1024,1024]{1,0:T(8,128)(2,1)S(1)} %shard_map.60.right.slope.slope_even), custom_call_target="tpu_custom_call" | custom-call | flops 1 | bytes 1 | tf_op jit(solution)/shard_map/pallas_call | solution.py:213
  203.6 3.6 %add_convert_fusion = bf16[768,1024]{1,0:T(8,128)(2,1)} fusion(f32[768,1024]{1,0:T(8,128)} %shard_map.61, bf16[768,1024]{1,0:T(8,128)(2,1)S(1)} %collective-permute-done.35), kind=kLoop, calls=%fused_computation.15 | loop fusion | flops 2359296 | bytes 6291456 | tf_op jit(solution)/shard_map/convert_element_type | solution.py:558
  210.8 3.3 %collective-permute-start.39 = (bf16[256,1024]{1,0:T(8,128)(2,1)S(1)}, bf16[256,1024]{1,0:T(8,128)(2,1)S(1)}, u32[]{:S(2)}, u32[]{:S(2)}) collective-permute-start(bf16[256,1024]{1,0:T(8,128)(2,1)S(1)} %get-tuple-element.221.refs_0_), channel_id=1, source_target_pairs={{0,48},{4,52},{8,56},{12,60},{16,0},{20,4},{24,8},{28,12},{32,16},... | collective-permute-start | bytes 1572872 | tf_op jit(solution)/shard_map/ppermute | solution.py:41
  226.6 3.2 %collective-permute-start.41 = (bf16[128,1024]{1,0:T(8,128)(2,1)S(1)}, bf16[128,1024]{1,0:T(8,128)(2,1)S(1)}, u32[]{:S(2)}, u32[]{:S(2)}) collective-permute-start(bf16[128,1024]{1,0:T(8,128)(2,1)S(1)} %get-tuple-element.232), channel_id=1, source_target_pairs={{0,12},{4,0},{8,4},{12,8},{16,28},{20,16},{24,20},{28,24},{32,44},... | collective-permute-start | bytes 786440 | tf_op jit(solution)/shard_map/ppermute | solution.py:41
  233.0 7.0 %shard_map.67.part = f32[768,1024]{1,0:T(8,128)} custom-call(bf16[768,2048]{1,0:T(8,128)(2,1)} %copy-done, bf16[768,2048]{1,0:T(8,128)(2,1)} %copy-done.2, bf16[1024,1024]{1,0:T(8,128)(2,1)S(1)} %shard_map.60.right.slope.slope_even, bf16[1024,1024]{1,0:T(8,128)(2,1)S(1)} %shard_map.62.right.slope.slope_odd), custom_call_target="tpu_custom_call" | custom-call | flops 1 | bytes 1 | tf_op jit(solution)/shard_map/pallas_call | solution.py:247
  246.4 4.0 %shard_map.69 = (f32[8,1024]{1,0:T(8,128)S(1)}, f32[8,1024]{1,0:T(8,128)S(1)}, bf16[1024,1024]{1,0:T(8,128)(2,1)S(1)}) custom-call(bf16[1024,1024]{1,0:T(8,128)(2,1)S(1)} %shard_map.68.slope, bf16[16,1024]{1,0:T(8,128)(2,1)S(1)} %broadcast_in_dim.41.weights, bf16[16,1024]{1,0:T(8,128)(2,1)S(1)} %broadcast_in_dim.44.means, ...), custom_call_target="tpu_custom_call", output_to_operand_aliasing={{2}: (0, {})} | custom-call | flops 1 | bytes 1 | tf_op jit(solution)/shard_map/pallas_call | solution.py:372
  255.6 8.8 %shard_map.72 = bf16[768,1024]{1,0:T(8,128)(2,1)} custom-call(bf16[768,2048]{1,0:T(8,128)(2,1)} %copy-done, bf16[768,2048]{1,0:T(8,128)(2,1)} %copy-done.2, bf16[1024,1024]{1,0:T(8,128)(2,1)} %copy-done.7, bf16[1024,1024]{1,0:T(8,128)(2,1)} %copy-done.8, f32[768,1024]{1,0:T(8,128)} %shard_map.67.part, bf16[768,1024]{1,0:T(8,128)(2,1)} %view.2, ...), custom_call_target="tpu_custom_call" | custom-call | flops 1 | bytes 1 | tf_op jit(solution)/shard_map/pallas_call | solution.py:247
  267.5 6.7 %shard_map.74 = bf16[768,1024]{1,0:T(8,128)(2,1)} custom-call(bf16[768,1024]{1,0:T(8,128)(2,1)} %copy-done.5, bf16[1024,1024]{1,0:T(8,128)(2,1)} %copy-done.7, bf16[768,1024]{1,0:T(8,128)(2,1)} %copy-done.16, bf16[768,1024]{1,0:T(8,128)(2,1)} %copy-done.15, bf16[768,1024]{1,0:T(8,128)(2,1)} %view.3, f32[8,1024]{1,0:T(8,128)} %concatenate.31.stats), custom_call_target="tpu_custom_call" | custom-call | flops 1 | bytes 1 | tf_op jit(solution)/shard_map/pallas_call | solution.py:288
  (205 shorter events, 136.8 us)
Async XLA Ops:
  0.7 36.4 %collective-permute-start = (bf16[768,1024]{1,0:T(8,128)(2,1)}, bf16[768,1024]{1,0:T(8,128)(2,1)}, u32[]{:S(2)}, u32[]{:S(2)}) collective-permute-start(bf16[768,1024]{1,0:T(8,128)(2,1)} %view.3), channel_id=1, source_target_pairs={{0,2},{1,3},{2,0},{3,1},{4,6},{5,7},{6,4},{7,5},{8,10},{9,11},{10,... | collective-permute-start | bytes 4718600 | tf_op jit(solution)/shard_map/ppermute | solution.py:41
  2.3 34.7 %collective-permute-start.1 = (bf16[768,1024]{1,0:T(8,128)(2,1)}, bf16[768,1024]{1,0:T(8,128)(2,1)S(1)}, u32[]{:S(2)}, u32[]{:S(2)}) collective-permute-start(bf16[768,1024]{1,0:T(8,128)(2,1)} %view.3), channel_id=1, source_target_pairs={{0,1},{1,0},{2,3},{3,2},{4,5},{5,4},{6,7},{7,6},{8,9},{9,8},{10,11... | collective-permute-start | bytes 4718600 | tf_op jit(solution)/shard_map/ppermute | solution.py:41
  60.9 17.3 %collective-permute-start.10 = (bf16[128,2048]{1,0:T(8,128)(2,1)}, bf16[128,2048]{1,0:T(8,128)(2,1)S(1)}, u32[]{:S(2)}, u32[]{:S(2)}) collective-permute-start(bf16[128,2048]{1,0:T(8,128)(2,1)} %get-tuple-element.153), channel_id=1, source_target_pairs={{0,48},{4,52},{8,56},{12,60},{16,0},{20,4},{24,8},{28,12},{32,16},... | collective-permute-start | bytes 1572872 | tf_op jit(solution)/shard_map/ppermute | solution.py:41
  64.0 16.6 %collective-permute-start.7 = (bf16[128,2048]{1,0:T(8,128)(2,1)}, bf16[128,2048]{1,0:T(8,128)(2,1)S(1)}, u32[]{:S(2)}, u32[]{:S(2)}) collective-permute-start(bf16[128,2048]{1,0:T(8,128)(2,1)} %get-tuple-element.150), channel_id=1, source_target_pairs={{0,4},{4,8},{8,12},{12,0},{16,20},{20,24},{24,28},{28,16},{32,36},... | collective-permute-start | bytes 1572872 | tf_op jit(solution)/shard_map/ppermute | solution.py:41
  65.9 14.6 %collective-permute-start.8 = (bf16[128,2048]{1,0:T(8,128)(2,1)}, bf16[128,2048]{1,0:T(8,128)(2,1)S(1)}, u32[]{:S(2)}, u32[]{:S(2)}) collective-permute-start(bf16[128,2048]{1,0:T(8,128)(2,1)} %get-tuple-element.151), channel_id=1, source_target_pairs={{0,12},{4,0},{8,4},{12,8},{16,28},{20,16},{24,20},{28,24},{32,44},... | collective-permute-start | bytes 1572872 | tf_op jit(solution)/shard_map/ppermute | solution.py:41
  68.1 15.3 %collective-permute-start.9 = (bf16[128,2048]{1,0:T(8,128)(2,1)}, bf16[128,2048]{1,0:T(8,128)(2,1)}, u32[]{:S(2)}, u32[]{:S(2)}) collective-permute-start(bf16[128,2048]{1,0:T(8,128)(2,1)} %get-tuple-element.152), channel_id=1, source_target_pairs={{0,16},{4,20},{8,24},{12,28},{16,32},{20,36},{24,40},{28,44},{32,4... | collective-permute-start | bytes 1572872 | tf_op jit(solution)/shard_map/ppermute | solution.py:41
  86.3 31.2 %collective-permute-start.11 = (bf16[256,2048]{1,0:T(8,128)(2,1)}, bf16[256,2048]{1,0:T(8,128)(2,1)}, u32[]{:S(2)}, u32[]{:S(2)}) collective-permute-start(bf16[256,2048]{1,0:T(8,128)(2,1)} %get-tuple-element.158), channel_id=1, source_target_pairs={{0,4},{4,8},{8,12},{12,0},{16,20},{20,24},{24,28},{28,16},{32,36},... | collective-permute-start | bytes 3145736 | tf_op jit(solution)/shard_map/ppermute | solution.py:41
  86.3 31.2 %collective-permute-start.12 = (bf16[256,2048]{1,0:T(8,128)(2,1)}, bf16[256,2048]{1,0:T(8,128)(2,1)}, u32[]{:S(2)}, u32[]{:S(2)}) collective-permute-start(bf16[256,2048]{1,0:T(8,128)(2,1)} %get-tuple-element.159), channel_id=1, source_target_pairs={{0,12},{4,0},{8,4},{12,8},{16,28},{20,16},{24,20},{28,24},{32,44},... | collective-permute-start | bytes 3145736 | tf_op jit(solution)/shard_map/ppermute | solution.py:41
  89.6 28.0 %collective-permute-start.13 = (bf16[256,2048]{1,0:T(8,128)(2,1)}, bf16[256,2048]{1,0:T(8,128)(2,1)}, u32[]{:S(2)}, u32[]{:S(2)}) collective-permute-start(bf16[256,2048]{1,0:T(8,128)(2,1)} %get-tuple-element.160), channel_id=1, source_target_pairs={{0,16},{4,20},{8,24},{12,28},{16,32},{20,36},{24,40},{28,44},{32,4... | collective-permute-start | bytes 3145736 | tf_op jit(solution)/shard_map/ppermute | solution.py:41
  89.6 28.0 %collective-permute-start.14 = (bf16[256,2048]{1,0:T(8,128)(2,1)}, bf16[256,2048]{1,0:T(8,128)(2,1)}, u32[]{:S(2)}, u32[]{:S(2)}) collective-permute-start(bf16[256,2048]{1,0:T(8,128)(2,1)} %get-tuple-element.161), channel_id=1, source_target_pairs={{0,48},{4,52},{8,56},{12,60},{16,0},{20,4},{24,8},{28,12},{32,16},... | collective-permute-start | bytes 3145736 | tf_op jit(solution)/shard_map/ppermute | solution.py:41
  98.4 19.2 %all-to-all-start.1 = ((f32[16,40,128]{2,1,0:T(8,128)}), f32[16,40,128]{2,1,0:T(8,128)S(1)}, u32[]{:S(2)}, u32[]{:S(2)}) async-start(f32[16,40,128]{2,1,0:T(8,128)} %broadcast_in_dim.40), calls=%async_computation.1 | async-start | bytes 655360 | tf_op jit(solution)/shard_map/all_to_all | solution.py:52
  170.5 15.8 %collective-permute-start.29 = (bf16[256,1024]{1,0:T(8,128)(2,1)S(1)}, bf16[256,1024]{1,0:T(8,128)(2,1)S(1)}, u32[]{:S(2)}, u32[]{:S(2)}) collective-permute-start(bf16[256,1024]{1,0:T(8,128)(2,1)S(1)} %get-tuple-element.206.refs_0_), channel_id=1, source_target_pairs={{0,8},{4,12},{8,0},{12,4},{16,24},{20,28},{24,16},{28,20},{32,40},... | collective-permute-start | bytes 1572872 | tf_op jit(solution)/shard_map/ppermute | solution.py:41
  171.7 20.1 %collective-permute-start.30 = (bf16[256,1024]{1,0:T(8,128)(2,1)S(1)}, bf16[256,1024]{1,0:T(8,128)(2,1)S(1)}, u32[]{:S(2)}, u32[]{:S(2)}) collective-permute-start(bf16[256,1024]{1,0:T(8,128)(2,1)S(1)} %get-tuple-element.206.refs_0_), channel_id=1, source_target_pairs={{0,4},{4,8},{8,12},{12,0},{16,20},{20,24},{24,28},{28,16},{32,36},... | collective-permute-start | bytes 1572872 | tf_op jit(solution)/shard_map/ppermute | solution.py:41
  174.3 18.4 %collective-permute-start.31 = (bf16[256,1024]{1,0:T(8,128)(2,1)S(1)}, bf16[256,1024]{1,0:T(8,128)(2,1)S(1)}, u32[]{:S(2)}, u32[]{:S(2)}) collective-permute-start(bf16[256,1024]{1,0:T(8,128)(2,1)S(1)} %get-tuple-element.206.refs_0_), channel_id=1, source_target_pairs={{0,12},{4,0},{8,4},{12,8},{16,28},{20,16},{24,20},{28,24},{32,44},... | collective-permute-start | bytes 1572872 | tf_op jit(solution)/shard_map/ppermute | solution.py:41
  174.9 17.8 %collective-permute-start.32 = (bf16[256,1024]{1,0:T(8,128)(2,1)S(1)}, bf16[256,1024]{1,0:T(8,128)(2,1)S(1)}, u32[]{:S(2)}, u32[]{:S(2)}) collective-permute-start(bf16[256,1024]{1,0:T(8,128)(2,1)S(1)} %get-tuple-element.209.refs_0_), channel_id=1, source_target_pairs={{0,32},{4,36},{8,40},{12,44},{16,48},{20,52},{24,56},{28,60},{32,0... | collective-permute-start | bytes 1572872 | tf_op jit(solution)/shard_map/ppermute | solution.py:41
  182.4 13.3 %collective-permute-start.33 = (bf16[256,1024]{1,0:T(8,128)(2,1)S(1)}, bf16[256,1024]{1,0:T(8,128)(2,1)S(1)}, u32[]{:S(2)}, u32[]{:S(2)}) collective-permute-start(bf16[256,1024]{1,0:T(8,128)(2,1)S(1)} %get-tuple-element.209.refs_0_), channel_id=1, source_target_pairs={{0,16},{4,20},{8,24},{12,28},{16,32},{20,36},{24,40},{28,44},{32,4... | collective-permute-start | bytes 1572872 | tf_op jit(solution)/shard_map/ppermute | solution.py:41
  207.2 44.6 %collective-permute-start.44 = (bf16[768,1024]{1,0:T(8,128)(2,1)}, bf16[768,1024]{1,0:T(8,128)(2,1)S(1)}, u32[]{:S(2)}, u32[]{:S(2)}) collective-permute-start(bf16[768,1024]{1,0:T(8,128)(2,1)} %add_convert_fusion), channel_id=1, source_target_pairs={{0,2},{1,3},{2,0},{3,1},{4,6},{5,7},{6,4},{7,5},{8,10},{9,11},{10,... | collective-permute-start | bytes 4718600 | tf_op jit(solution)/shard_map/ppermute | solution.py:41
  207.4 15.4 %collective-permute-start.36 = (bf16[256,1024]{1,0:T(8,128)(2,1)S(1)}, bf16[256,1024]{1,0:T(8,128)(2,1)S(1)}, u32[]{:S(2)}, u32[]{:S(2)}) collective-permute-start(bf16[256,1024]{1,0:T(8,128)(2,1)S(1)} %get-tuple-element.219.refs_0_), channel_id=1, source_target_pairs={{0,4},{4,8},{8,12},{12,0},{16,20},{20,24},{24,28},{28,16},{32,36},... | collective-permute-start | bytes 1572872 | tf_op jit(solution)/shard_map/ppermute | solution.py:41
  209.4 13.8 %collective-permute-start.37 = (bf16[256,1024]{1,0:T(8,128)(2,1)S(1)}, bf16[256,1024]{1,0:T(8,128)(2,1)S(1)}, u32[]{:S(2)}, u32[]{:S(2)}) collective-permute-start(bf16[256,1024]{1,0:T(8,128)(2,1)S(1)} %get-tuple-element.219.refs_0_), channel_id=1, source_target_pairs={{0,12},{4,0},{8,4},{12,8},{16,28},{20,16},{24,20},{28,24},{32,44},... | collective-permute-start | bytes 1572872 | tf_op jit(solution)/shard_map/ppermute | solution.py:41
  210.6 15.6 %collective-permute-start.38 = (bf16[256,1024]{1,0:T(8,128)(2,1)S(1)}, bf16[256,1024]{1,0:T(8,128)(2,1)S(1)}, u32[]{:S(2)}, u32[]{:S(2)}) collective-permute-start(bf16[256,1024]{1,0:T(8,128)(2,1)S(1)} %get-tuple-element.221.refs_0_), channel_id=1, source_target_pairs={{0,16},{4,20},{8,24},{12,28},{16,32},{20,36},{24,40},{28,44},{32,4... | collective-permute-start | bytes 1572872 | tf_op jit(solution)/shard_map/ppermute | solution.py:41
  210.8 15.4 %collective-permute-start.39 = (bf16[256,1024]{1,0:T(8,128)(2,1)S(1)}, bf16[256,1024]{1,0:T(8,128)(2,1)S(1)}, u32[]{:S(2)}, u32[]{:S(2)}) collective-permute-start(bf16[256,1024]{1,0:T(8,128)(2,1)S(1)} %get-tuple-element.221.refs_0_), channel_id=1, source_target_pairs={{0,48},{4,52},{8,56},{12,60},{16,0},{20,4},{24,8},{28,12},{32,16},... | collective-permute-start | bytes 1572872 | tf_op jit(solution)/shard_map/ppermute | solution.py:41
  226.5 13.5 %collective-permute-start.40 = (bf16[128,1024]{1,0:T(8,128)(2,1)S(1)}, bf16[128,1024]{1,0:T(8,128)(2,1)S(1)}, u32[]{:S(2)}, u32[]{:S(2)}) collective-permute-start(bf16[128,1024]{1,0:T(8,128)(2,1)S(1)} %get-tuple-element.231), channel_id=1, source_target_pairs={{0,4},{4,8},{8,12},{12,0},{16,20},{20,24},{24,28},{28,16},{32,36},... | collective-permute-start | bytes 786440 | tf_op jit(solution)/shard_map/ppermute | solution.py:41
  226.6 13.4 %collective-permute-start.41 = (bf16[128,1024]{1,0:T(8,128)(2,1)S(1)}, bf16[128,1024]{1,0:T(8,128)(2,1)S(1)}, u32[]{:S(2)}, u32[]{:S(2)}) collective-permute-start(bf16[128,1024]{1,0:T(8,128)(2,1)S(1)} %get-tuple-element.232), channel_id=1, source_target_pairs={{0,12},{4,0},{8,4},{12,8},{16,28},{20,16},{24,20},{28,24},{32,44},... | collective-permute-start | bytes 786440 | tf_op jit(solution)/shard_map/ppermute | solution.py:41
  251.9 14.4 %collective-permute-start.48 = (bf16[768,1024]{1,0:T(8,128)(2,1)}, bf16[768,1024]{1,0:T(8,128)(2,1)S(1)}, u32[]{:S(2)}, u32[]{:S(2)}) collective-permute-start(bf16[768,1024]{1,0:T(8,128)(2,1)} %shard_map.73), channel_id=1, source_target_pairs={{0,1},{1,0},{2,3},{3,2},{4,5},{5,4},{6,7},{7,6},{8,9},{9,8},{10,11... | collective-permute-start | bytes 4718600 | tf_op jit(solution)/shard_map/ppermute | solution.py:41
  (43 other events, 319.9 us)
